TPU v7x, 32 devices: a whole 2x2x4 slice. The times are simulated.
32 devices in a mesh: fsdp: 8 (over z, x), dp: 4 (over y, core).
Axes of the slice: x: 2, y: 2, z: 4, core: 2. Of those that a mesh axis runs over, the one named last changes fastest.
Arguments:
- tokens: bfloat16 [64, 237, 768], P(('fsdp', 'dp')), may hold values from -6 to 6
- token_type: int32 [64, 237], P(('fsdp', 'dp')), may hold values from 0 to 1, as said below
- mlm_mask: int32 [64, 237], P(('fsdp', 'dp')), may hold values from 0 to 1, as said below
- cotangent: bfloat16 [64, 237, 768], P(('fsdp', 'dp')), may hold values from -6 to 6
- ln1_gain: bfloat16 [768], P('fsdp'), may hold values from 0.5 to 1.5
- ln1_bias: bfloat16 [768], P('fsdp'), may hold values from -2 to 2
- w_qkv: bfloat16 [768, 2304], P('fsdp'), may hold values from -0.21875 to 0.21875
- w_out: bfloat16 [768, 768], P('fsdp'), may hold values from -0.875 to 0.875
- ln2_gain: bfloat16 [768], P('fsdp'), may hold values from 0.5 to 1.5
- ln2_bias: bfloat16 [768], P('fsdp'), may hold values from -2 to 2
- w_up: bfloat16 [2, 768, 3072], P(None, 'fsdp'), may hold values from -0.21875 to 0.21875
- w_down: bfloat16 [2, 3072, 768], P(None, None, 'fsdp'), may hold values from -0.109375 to 0.109375
Outputs:
- mixed: bfloat16 [64, 237, 768], P(('fsdp', 'dp'))
- input_grad: float32 [64, 237, 768], P(('fsdp', 'dp'))
- ln1_gain_grad: float32 [768], P('fsdp')
- ln1_bias_grad: float32 [768], P('fsdp')
- qkv_grad: float32 [768, 2304], P('fsdp')
- out_grad: float32 [768, 768], P('fsdp')
- ln2_gain_grad: float32 [768], P('fsdp')
- ln2_bias_grad: float32 [768], P('fsdp')
- up_grad: float32 [2, 768, 3072], P(None, 'fsdp')
- down_grad: float32 [2, 3072, 768], P(None, None, 'fsdp')
- expert_counts: int32 [2], replicated
Inputs may be any that keep to these rules, and one draw needn't show every extreme that they name: `token_type`: in each sequence, 1 marks exactly the first 197 positions (an image-caption pair) or no position (a text-only sequence); sequence 0 is a pair. `mlm_mask`: the last position of every sequence is 1, and so is the first position of sequence 0.
All inputs are finite; a program needn't handle non-finite values.
Results may differ from a plain program's by a relative error of at most 0.012.
Values may be sent and summed in bfloat16 or wider, within the bound.
No kernel may reach another device: no remote copies, remote signals or barrier semaphores. Data moves between devices by JAX's collectives and lax.ppermute only.
A program may use at most 320 MiB of HBM per device.

v0:
```python
import jax
import jax.numpy as jnp
from jax import lax
from jax.sharding import PartitionSpec as P

HEADS = 12
HEAD = 64


def normalize(values, gain_vec, bias_vec):
    center = values - jnp.mean(values, -1, keepdims=True)
    spread = jnp.mean(center * center, -1, keepdims=True)
    return center * lax.rsqrt(spread + 1e-06) * gain_vec + bias_vec


def gelu_exact(values):
    return jax.nn.gelu(values, approximate=False)


def contract_last(left, right):
    return lax.dot_general(
        left, right, (((1,), (1,)), ((), ())), preferred_element_type=jnp.float32
    )


def contract_first(left, right):
    return lax.dot_general(
        left, right, (((0,), (0,)), ((), ())), preferred_element_type=jnp.float32
    )


def attention_scores(query_part, key_part, score_scale):
    return (
        jnp.einsum("sqhe,skhe->shqk", query_part, key_part, preferred_element_type=jnp.float32)
        * score_scale
    )


def per_device(
    tokens,
    token_type,
    mlm_mask,
    cotangent,
    ln1_gain,
    ln1_bias,
    w_qkv,
    w_out,
    ln2_gain,
    ln2_bias,
    w_up,
    w_down,
):
    sequences, positions, model_width = tokens.shape
    row_count = sequences * positions
    score_scale = HEAD ** (-0.5)
    inputs = tokens.astype(jnp.float32).reshape(row_count, model_width)
    attn_full = (
        lax.all_gather(ln1_gain, "fsdp", axis=0, tiled=True),
        lax.all_gather(ln1_bias, "fsdp", axis=0, tiled=True),
        lax.all_gather(w_qkv, "fsdp", axis=0, tiled=True),
        lax.all_gather(w_out, "fsdp", axis=0, tiled=True),
    )
    gain_one = attn_full[0].astype(jnp.float32)
    bias_one = attn_full[1].astype(jnp.float32)
    first_in = normalize(inputs, gain_one, bias_one).astype(jnp.bfloat16)
    qkv_all = jnp.dot(first_in, attn_full[2], preferred_element_type=jnp.float32).astype(
        jnp.bfloat16
    )
    qkv_all = qkv_all.reshape(sequences, positions, 3, HEADS, HEAD)
    query_part = qkv_all[:, :, 0]
    key_part = qkv_all[:, :, 1]
    value_part = qkv_all[:, :, 2]
    scores = attention_scores(query_part, key_part, score_scale)
    row_max = jnp.max(scores, -1, keepdims=True)
    log_total = row_max + jnp.log(jnp.sum(jnp.exp(scores - row_max), -1, keepdims=True))
    attn_low = jnp.exp(scores - log_total).astype(jnp.bfloat16)
    context = jnp.einsum(
        "shqk,skhe->sqhe", attn_low, value_part, preferred_element_type=jnp.float32
    )
    context = context.reshape(row_count, model_width).astype(jnp.bfloat16)
    hidden = inputs + jnp.dot(context, attn_full[3], preferred_element_type=jnp.float32)
    ffn_full = (
        lax.all_gather(ln2_gain, "fsdp", axis=0, tiled=True),
        lax.all_gather(ln2_bias, "fsdp", axis=0, tiled=True),
        lax.all_gather(w_up, "fsdp", axis=1, tiled=True),
        lax.all_gather(w_down, "fsdp", axis=2, tiled=True),
    )
    gain_two = ffn_full[0].astype(jnp.float32)
    bias_two = ffn_full[1].astype(jnp.float32)
    second_in = normalize(hidden, gain_two, bias_two).astype(jnp.bfloat16)
    token_kinds = token_type.reshape(row_count)
    language = 1 - token_kinds
    block_rows = 128
    padded_rows = (row_count // block_rows + 2) * block_rows
    block_count = padded_rows // block_rows
    lang_blocks = (jnp.sum(language) + block_rows - 1) // block_rows
    row_slot = jnp.where(
        token_kinds == 1,
        lang_blocks * block_rows + jnp.cumsum(token_kinds) - 1,
        jnp.cumsum(language) - 1,
    )
    block_expert = (jnp.arange(block_count) >= lang_blocks).astype(jnp.int32)
    padded_in = jnp.zeros((padded_rows, model_width), jnp.bfloat16).at[row_slot].set(second_in)
    padded_in = padded_in.reshape(block_count, block_rows, model_width)
    up_full = ffn_full[2]
    down_full = ffn_full[3]

    def expert_forward(unused, block_item):
        block_in, expert = block_item
        pre_act = jnp.dot(block_in, up_full[expert], preferred_element_type=jnp.float32)
        post_act = gelu_exact(pre_act).astype(jnp.bfloat16)
        return (
            unused,
            (pre_act, jnp.dot(post_act, down_full[expert], preferred_element_type=jnp.float32)),
        )

    unused, (pre_blocks, out_blocks) = lax.scan(expert_forward, 0, (padded_in, block_expert))
    branch = out_blocks.reshape(padded_rows, model_width)[row_slot]
    mixed = (hidden + branch).astype(jnp.bfloat16).reshape(sequences, positions, model_width)
    masked = mlm_mask.reshape(row_count).astype(jnp.float32)
    kinds_float = token_kinds.astype(jnp.float32)
    local_counts = jnp.stack([jnp.sum(masked * (1.0 - kinds_float)), jnp.sum(masked * kinds_float)])
    totals = lax.psum(local_counts, ("fsdp", "dp"))
    ffn_back = (
        lax.all_gather(ln2_gain, "fsdp", axis=0, tiled=True),
        lax.all_gather(ln2_bias, "fsdp", axis=0, tiled=True),
        lax.all_gather(w_up, "fsdp", axis=1, tiled=True),
        lax.all_gather(w_down, "fsdp", axis=2, tiled=True),
    )
    up_back = ffn_back[2]
    down_back = ffn_back[3]
    out_low = (
        (cotangent.astype(jnp.float32) * mlm_mask[..., None].astype(jnp.float32))
        .reshape(row_count, model_width)
        .astype(jnp.bfloat16)
    )
    padded_grad = jnp.zeros((padded_rows, model_width), jnp.bfloat16).at[row_slot].set(out_low)
    padded_grad = padded_grad.reshape(block_count, block_rows, model_width)

    def expert_backward(totals_now, block_item):
        up_total, down_total = totals_now
        block_in, block_grad, pre_act, expert = block_item
        post_act, gelu_back = jax.vjp(gelu_exact, pre_act)
        act_low = post_act.astype(jnp.bfloat16)
        act_grad = contract_last(block_grad, down_back[expert])
        pre_grad = gelu_back(act_grad)[0].astype(jnp.bfloat16)
        in_grad = contract_last(pre_grad, up_back[expert])
        down_total = down_total.at[expert].add(contract_first(act_low, block_grad))
        up_total = up_total.at[expert].add(contract_first(block_in, pre_grad))
        return ((up_total, down_total), in_grad)

    start_totals = (
        jnp.zeros((2, model_width, up_back.shape[2]), jnp.float32),
        jnp.zeros((2, down_back.shape[1], model_width), jnp.float32),
    )
    (up_raw, down_raw), in_blocks = lax.scan(
        expert_backward, start_totals, (padded_in, padded_grad, pre_blocks, block_expert)
    )
    second_grad = in_blocks.reshape(padded_rows, model_width)[row_slot]
    unused_two, norm_back_two = jax.vjp(normalize, hidden, gain_two, bias_two)
    hidden_part, gain_two_grad, bias_two_grad = norm_back_two(second_grad)
    hidden_grad = out_low.astype(jnp.float32) + hidden_part
    attn_back = (
        lax.all_gather(ln1_gain, "fsdp", axis=0, tiled=True),
        lax.all_gather(ln1_bias, "fsdp", axis=0, tiled=True),
        lax.all_gather(w_qkv, "fsdp", axis=0, tiled=True),
        lax.all_gather(w_out, "fsdp", axis=0, tiled=True),
    )
    hidden_low = hidden_grad.astype(jnp.bfloat16)
    out_weight_grad = contract_first(context, hidden_low)
    context_grad = contract_last(hidden_low, attn_back[3]).astype(jnp.bfloat16)
    context_grad = context_grad.reshape(sequences, positions, HEADS, HEAD)
    attn_probs = jnp.exp(attention_scores(query_part, key_part, score_scale) - log_total)
    prob_grad = jnp.einsum(
        "sqhe,skhe->shqk", context_grad, value_part, preferred_element_type=jnp.float32
    )
    score_grad = (
        attn_probs * (prob_grad - jnp.sum(prob_grad * attn_probs, -1, keepdims=True))
    ).astype(jnp.bfloat16)
    query_grad = (
        jnp.einsum("shqk,skhe->sqhe", score_grad, key_part, preferred_element_type=jnp.float32)
        * score_scale
    )
    key_grad = (
        jnp.einsum("shqk,sqhe->skhe", score_grad, query_part, preferred_element_type=jnp.float32)
        * score_scale
    )
    value_grad = jnp.einsum(
        "shqk,sqhe->skhe",
        attn_probs.astype(jnp.bfloat16),
        context_grad,
        preferred_element_type=jnp.float32,
    )
    qkv_grad_low = (
        jnp.stack([query_grad, key_grad, value_grad], 2)
        .astype(jnp.bfloat16)
        .reshape(row_count, 3 * model_width)
    )
    qkv_weight_grad = contract_first(first_in, qkv_grad_low)
    first_grad = contract_last(qkv_grad_low, attn_back[2])
    unused_one, norm_back_one = jax.vjp(normalize, inputs, gain_one, bias_one)
    input_part, gain_one_grad, bias_one_grad = norm_back_one(first_grad)
    input_grad = (hidden_grad + input_part).reshape(sequences, positions, model_width)
    attn_sums = (
        lax.psum_scatter(gain_one_grad, "fsdp", scatter_dimension=0, tiled=True),
        lax.psum_scatter(bias_one_grad, "fsdp", scatter_dimension=0, tiled=True),
        lax.psum_scatter(qkv_weight_grad, "fsdp", scatter_dimension=0, tiled=True),
        lax.psum_scatter(out_weight_grad, "fsdp", scatter_dimension=0, tiled=True),
    )
    ffn_sums = (
        lax.psum_scatter(gain_two_grad, "fsdp", scatter_dimension=0, tiled=True),
        lax.psum_scatter(bias_two_grad, "fsdp", scatter_dimension=0, tiled=True),
        lax.psum_scatter(up_raw, "fsdp", scatter_dimension=1, tiled=True),
        lax.psum_scatter(down_raw, "fsdp", scatter_dimension=2, tiled=True),
    )
    gains = lax.psum((attn_sums[0], attn_sums[1], ffn_sums[0], ffn_sums[1]), "dp")
    parts = (
        lax.psum_scatter(attn_sums[2], "dp", scatter_dimension=1, tiled=True),
        lax.psum_scatter(attn_sums[3], "dp", scatter_dimension=1, tiled=True),
        lax.psum_scatter(ffn_sums[2], "dp", scatter_dimension=2, tiled=True),
        lax.psum_scatter(ffn_sums[3], "dp", scatter_dimension=1, tiled=True),
    )
    whole = (
        lax.all_gather(parts[0], "dp", axis=1, tiled=True),
        lax.all_gather(parts[1], "dp", axis=1, tiled=True),
        lax.all_gather(parts[2], "dp", axis=2, tiled=True),
        lax.all_gather(parts[3], "dp", axis=1, tiled=True),
    )
    divisor = totals[:, None, None]
    up_grad = whole[2] / divisor
    down_grad = whole[3] / divisor
    return (
        mixed,
        input_grad,
        gains[0],
        gains[1],
        whole[0],
        whole[1],
        gains[2],
        gains[3],
        up_grad,
        down_grad,
        totals.astype(jnp.int32),
    )


def solution(mesh):
    return jax.shard_map(
        per_device,
        mesh=mesh,
        in_specs=(
            P(("fsdp", "dp"), None, None),
            P(("fsdp", "dp"), None),
            P(("fsdp", "dp"), None),
            P(("fsdp", "dp"), None, None),
            P("fsdp"),
            P("fsdp"),
            P("fsdp", None),
            P("fsdp", None),
            P("fsdp"),
            P("fsdp"),
            P(None, "fsdp", None),
            P(None, None, "fsdp"),
        ),
        out_specs=(
            P(("fsdp", "dp"), None, None),
            P(("fsdp", "dp"), None, None),
            P("fsdp"),
            P("fsdp"),
            P("fsdp", None),
            P("fsdp", None),
            P("fsdp"),
            P("fsdp"),
            P(None, "fsdp", None),
            P(None, None, "fsdp"),
            P(),
        ),
        check_vma=False,
    )
```

profile of v0, /device:TPU:0, one launch (start us, length us, event | category | flops | bytes accessed | tf_op | source)
XLA Modules:
  0.0 1869.8 jit_solution(10924851944854443880)
XLA Ops:
  16.5 23.8 %all-reduce.12 = (bf16[768]{0:T(1024)(128)(2,1)S(1)}, bf16[768]{0:T(1024)(128)(2,1)S(1)}, bf16[768]{0:T(1024)(128)(2,1)S(1)}, bf16[768]{0:T(1024)(128)(2,1)S(1)}) all-reduce(bf16[768]{0:T(1024)(128)(2,1)S(1)} %dynamic-update-slice.7, bf16[768]{0:T(1024)(128)(2,1)S(1)} %dynamic-update-slice.6, ...), channel_id=1, replica_groups=mesh['fsdp'=8,'dp'=4] {'fsdp'}, use_global_device_ids=true, to_apply=%add.3 | all-reduce | flops 3072 | bytes 12288
  52.6 26.1 %all-gather.8.cloned.1.call-done = bf16[768,2304]{1,0:T(8,128)(2,1)} async-done(((bf16[96,2304]{1,0:T(8,128)(2,1)}), bf16[768,2304]{1,0:T(8,128)(2,1)}) %all-gather.8.cloned.1.call-update) | async-done | bytes 3538960 | tf_op jit(solution)/shard_map/all_gather | solution.py:60
  105.5 15.0 all-gather.10.cloned.1.call-done
  126.3 133.8 %all-gather.14.cloned.1.call-done = bf16[2,3072,768]{1,0,2:T(2,128)(2,1)} async-done(((bf16[2,3072,96]{1,0,2:T(2,128)(2,1)}), bf16[2,3072,768]{1,0,2:T(2,128)(2,1)}) %all-gather.14.cloned.1.call-update) | async-done | bytes 9437200 | tf_op jit(solution)/shard_map/all_gather | solution.py:86
  260.1 23.7 %copy.102 = bf16[2,3072,768]{2,1,0:T(8,128)(2,1)} copy(bf16[2,3072,768]{1,0,2:T(2,128)(2,1)} %all-gather.14.cloned.1.call-done) | data formatting | bytes 18874368 | tf_op jit(solution)/shard_map/while | solution.py:117
  283.8 114.6 %all-gather.12.cloned.1.call-done = bf16[2,768,3072]{2,1,0:T(8,128)(2,1)} async-done(((bf16[2,96,3072]{2,1,0:T(8,128)(2,1)}), bf16[2,768,3072]{2,1,0:T(8,128)(2,1)}) %all-gather.12.cloned.1.call-update) | async-done | bytes 9437200 | tf_op jit(solution)/shard_map/all_gather | solution.py:85
  398.6 63.6 %while.28 = (s32[]{:T(128)}, f32[5,128,3072]{2,1,0:T(8,128)}, f32[5,128,768]{2,1,0:T(8,128)S(1)}, bf16[5,128,768]{2,1,0:T(8,128)(2,1)S(1)}, s32[5]{0:T(128)S(1)}...) while((s32[]{:T(128)}, f32[5,128,3072]{2,1,0:T(8,128)}, ...), condition=%wide.region_13.14_spmd, body=%wide.region_12.13_spmd.sunk | while | flops 1233518592 | bytes 14747291 | solution.py:117
  480.6 352.0 %while.29 = (s32[]{:T(128)}, f32[2,768,3072]{2,1,0:T(8,128)}, f32[2,3072,768]{1,2,0:T(8,128)}, f32[5,128,768]{2,1,0:T(8,128)S(1)}, s32[5]{0:T(128)S(1)}, /*index...) while((s32[]{:T(128)}, f32[2,768,3072]{2,1,0:T(8,128)}, ...), condition=%wide.region_17.18_spmd, body=%wide.region_15.17_spmd.sunk | while | flops 2479226880 | bytes 157488432 | solution.py:156
  502.9 9.6 copy.175
  512.5 10.2 add_select_fusion.3
  522.6 9.6 copy.176
  571.2 9.6 copy.175
  580.8 10.2 add_select_fusion.3
  591.0 9.6 copy.176
  639.5 9.6 copy.175
  649.1 10.2 add_select_fusion.3
  659.3 9.6 copy.176
  707.8 9.6 copy.175
  717.4 10.2 add_select_fusion.3
  727.5 9.6 copy.176
  776.0 9.6 copy.175
  785.6 10.2 add_select_fusion.3
  795.8 9.6 copy.176
  887.8 256.3 %reduce-scatter.21.cloned.1.call-done = f32[2,3072,96]{1,2,0:T(8,128)} async-done(((f32[2,3072,768]{1,2,0:T(8,128)}), f32[2,3072,96]{1,2,0:T(8,128)}) %reduce-scatter.21.cloned.1.call-update) | async-done | bytes 2359312 | tf_op jit(solution)/shard_map/reduce_scatter | solution.py:214
  1144.2 316.1 %reduce-scatter.17.cloned.1.call-done = f32[2,96,3072]{2,1,0:T(8,128)} async-done(((f32[2,768,3072]{2,1,0:T(8,128)}), f32[2,96,3072]{2,1,0:T(8,128)}) %reduce-scatter.17.cloned.1.call-update) | async-done | bytes 2359312 | tf_op jit(solution)/shard_map/reduce_scatter | solution.py:213
  1460.4 71.6 %reduce-scatter.15.cloned.1.call-done = f32[96,768]{1,0:T(8,128)} async-done(((f32[768,768]{1,0:T(8,128)}), f32[96,768]{1,0:T(8,128)}) %reduce-scatter.15.cloned.1.call-update) | async-done | bytes 294928 | tf_op jit(solution)/shard_map/reduce_scatter | solution.py:208
  1533.9 129.8 %reduce-scatter.13.cloned.1.call-done = f32[96,2304]{1,0:T(8,128)} async-done(((f32[768,2304]{1,0:T(8,128)}), f32[96,2304]{1,0:T(8,128)}) %reduce-scatter.13.cloned.1.call-update) | async-done | bytes 884752 | tf_op jit(solution)/shard_map/reduce_scatter | solution.py:207
  1666.5 32.2 %reduce-scatter.23.cloned.1.call-done = f32[2,768,96]{1,2,0:T(8,128)} async-done(((f32[2,3072,96]{1,2,0:T(8,128)}), f32[2,768,96]{1,2,0:T(8,128)}) %reduce-scatter.23.cloned.1.call-update) | async-done | bytes 589840 | tf_op jit(solution)/shard_map/reduce_scatter | solution.py:221
  1698.7 35.4 %reduce-scatter.19.cloned.1.call-done = f32[2,96,768]{2,1,0:T(8,128)} async-done(((f32[2,96,3072]{2,1,0:T(8,128)}), f32[2,96,768]{2,1,0:T(8,128)}) %reduce-scatter.19.cloned.1.call-update) | async-done | bytes 589840 | tf_op jit(solution)/shard_map/reduce_scatter | solution.py:220
  1736.1 39.3 %psum.39 = f32[2]{0:T(128)S(1)} all-reduce(f32[2]{0:T(128)S(1)} %pad_maximum_fusion), channel_id=1, replica_groups=mesh['fsdp'=8,'dp'=4] {'fsdp','dp'}, use_global_device_ids=true, to_apply=%region_43.44 | all-reduce | flops 2 | bytes 16 | tf_op jit(solution)/shard_map/psum | solution.py:123
  1782.9 36.9 %all-reduce.10 = (f32[768]{0:T(1024)S(1)}, f32[768]{0:T(1024)S(1)}, f32[768]{0:T(1024)S(1)}, f32[768]{0:T(1024)S(1)}) all-reduce(f32[768]{0:T(1024)S(1)} %get-tuple-element.212, f32[768]{0:T(1024)S(1)} %get-tuple-element.215, f32[768]{0:T(1024)S(1)} %get-tuple-element.210, ...), channel_id=2, replica_groups=mesh['fsdp'=8,'dp'=4] {'fsdp'}, use_global_device_ids=true, to_apply=%region_24.25.clone | all-reduce | flops 3072 | bytes 24576
  1844.3 9.8 all-gather
  (356 shorter events, 411.4 us)
Async XLA Ops:
  7.2 71.5 %all-gather.8.cloned.1.call-start = ((), (), s32[]{:S(2)}) async-start(), calls=%async_computation.8 | async-start | bytes 3981312 | tf_op jit(solution)/shard_map/all_gather | solution.py:60
  7.9 112.6 %all-gather.10.cloned.1.call-start = ((), (), s32[]{:S(2)}) async-start(), calls=%async_computation.9 | async-start | bytes 1327104 | tf_op jit(solution)/shard_map/all_gather | solution.py:61
  8.7 251.4 %all-gather.14.cloned.1.call-start = ((), (), s32[]{:S(2)}) async-start(), calls=%async_computation.11 | async-start | bytes 10616832 | tf_op jit(solution)/shard_map/all_gather | solution.py:86
  12.2 28.1 %copy-start.7 = (bf16[2,237,768]{2,0,1:T(2,128)(2,1)S(1)}, bf16[2,237,768]{2,0,1:T(2,128)(2,1)}, u32[]{:S(2)}) copy-start(bf16[2,237,768]{2,0,1:T(2,128)(2,1)} %param.20) | copy-start | bytes 2184196
  12.3 386.2 %all-gather.12.cloned.1.call-start = ((), (), s32[]{:S(2)}) async-start(), calls=%async_computation.10 | async-start | bytes 10616832 | tf_op jit(solution)/shard_map/all_gather | solution.py:85
  12.9 1131.2 %reduce-scatter.21.cloned.1.call-start = ((), (), s32[]{:S(2)}) async-start(), calls=%async_computation.17 | async-start | bytes 21233664 | tf_op jit(solution)/shard_map/reduce_scatter | solution.py:214
  40.4 38.3 %copy-start.31 = (f32[768]{0:T(1024)}, f32[768]{0:T(1024)S(1)}, u32[]{:S(2)}) copy-start(f32[768]{0:T(1024)S(1)} %convert_element_type.111) | copy-start | bytes 9220
  40.4 38.3 %copy-start.41 = (f32[768]{0:T(1024)}, f32[768]{0:T(1024)S(1)}, u32[]{:S(2)}) copy-start(f32[768]{0:T(1024)S(1)} %convert_element_type.112) | copy-start | bytes 9220
  45.0 33.7 %copy-start.44 = (f32[474]{0:T(512)}, f32[474]{0:T(512)S(1)}, u32[]{:S(2)}) copy-start(f32[474]{0:T(512)S(1)} %rsqrt.25) | copy-start | bytes 5692
  45.1 33.6 %copy-start.46 = (f32[474]{0:T(512)}, f32[474]{0:T(512)S(1)}, u32[]{:S(2)}) copy-start(f32[474]{0:T(512)S(1)} %div.67) | copy-start | bytes 5692
  46.7 73.8 %copy-start.4 = (f32[474,768]{1,0:T(8,128)}, f32[474,768]{1,0:T(8,128)S(1)}, u32[]{:S(2)}) copy-start(f32[474,768]{1,0:T(8,128)S(1)} %reshape.279) | copy-start | bytes 4368388
  47.6 75.6 %copy-start.27 = (f32[768]{0:T(1024)}, f32[768]{0:T(1024)S(1)}, u32[]{:S(2)}) copy-start(f32[768]{0:T(1024)S(1)} %convert_element_type.119) | copy-start | bytes 9220
  48.7 35.4 %copy-start.16 = (bf16[474,768]{1,0:T(8,128)(2,1)}, bf16[474,768]{1,0:T(8,128)(2,1)S(1)}, u32[]{:S(2)}) copy-start(bf16[474,768]{1,0:T(8,128)(2,1)S(1)} %reshape.321) | copy-start | bytes 2184196
  49.0 74.2 %copy-start.49 = (s32[474]{0:T(512)}, s32[474]{0:T(512)S(1)}, u32[]{:S(2)}) copy-start(s32[474]{0:T(512)S(1)} %compare_select_fusion) | copy-start | bytes 5692
  123.2 160.6 %copy-start.35 = (f32[474]{0:T(512)}, f32[474]{0:T(512)S(1)}, u32[]{:S(2)}) copy-start(f32[474]{0:T(512)S(1)} %multiply_reduce_fusion.6) | copy-start | bytes 5692
  123.2 160.6 %copy-start.33 = (f32[474]{0:T(512)}, f32[474]{0:T(512)S(1)}, u32[]{:S(2)}) copy-start(f32[474]{0:T(512)S(1)} %fusion.225) | copy-start | bytes 5692
  532.2 25.6 %slice-start = ((s8[9437184]{0:T(1024)(128)(4,1)}), s8[1048576]{0:T(1024)(128)(4,1)S(1)}, s32[]{:S(2)}) async-start(s8[9437184]{0:T(1024)(128)(4,1)} %bitcast.245), calls=%async_computation.22 | async-start | bytes 2097152 | tf_op jit(solution)/shard_map/while
  832.6 627.7 %reduce-scatter.17.cloned.1.call-start = ((), (), s32[]{:S(2)}) async-start(), calls=%async_computation.14 | async-start | bytes 21233664 | tf_op jit(solution)/shard_map/reduce_scatter | solution.py:213
  833.2 698.8 %reduce-scatter.15.cloned.1.call-start = ((), (), s32[]{:S(2)}) async-start(), calls=%async_computation.13 | async-start | bytes 2654208 | tf_op jit(solution)/shard_map/reduce_scatter | solution.py:208
  848.2 815.5 %reduce-scatter.13.cloned.1.call-start = ((), (), s32[]{:S(2)}) async-start(), calls=%async_computation.12 | async-start | bytes 7962624 | tf_op jit(solution)/shard_map/reduce_scatter | solution.py:207
  887.7 810.9 %reduce-scatter.23.cloned.1.call-start = ((), (), s32[]{:S(2)}) async-start(), calls=%async_computation.18 | async-start | bytes 2949120 | tf_op jit(solution)/shard_map/reduce_scatter | solution.py:221
  1144.1 590.0 %reduce-scatter.19.cloned.1.call-start = ((), (), s32[]{:S(2)}) async-start(), calls=%async_computation.15 | async-start | bytes 2949120 | tf_op jit(solution)/shard_map/reduce_scatter | solution.py:220
  1460.3 375.4 %reduce-scatter.27.cloned.1.call-start = ((), (), s32[]{:S(2)}) async-start(), calls=%async_computation.21 | async-start | bytes 491520
  1533.9 309.4 %reduce-scatter.25.cloned.1.call-start = ((), (), s32[]{:S(2)}) async-start(), calls=%async_computation.20 | async-start | bytes 1474560
  1666.4 67.8 %copy-start.38 = (s32[2,237]{1,0:T(2,128)S(1)}, s32[2,237]{1,0:T(2,128)}, u32[]{:S(2)}) copy-start(s32[2,237]{1,0:T(2,128)} %param.21) | copy-start | bytes 5692
  1666.4 67.8 %copy-start.52 = (s32[2,237]{1,0:T(2,128)S(1)}, s32[2,237]{1,0:T(2,128)}, u32[]{:S(2)}) copy-start(s32[2,237]{1,0:T(2,128)} %param.22) | copy-start | bytes 5692
  1666.4 110.2 %copy-start.5 = (f32[474,768]{1,0:T(8,128)S(1)}, f32[474,768]{1,0:T(8,128)}, u32[]{:S(2)}) copy-start(f32[474,768]{1,0:T(8,128)} %copy-done.4) | copy-start | bytes 4368388
  1666.4 110.2 %copy-start.45 = (f32[474]{0:T(512)S(1)}, f32[474]{0:T(512)}, u32[]{:S(2)}) copy-start(f32[474]{0:T(512)} %copy-done.44) | copy-start | bytes 5692
  1666.4 110.2 %copy-start.47 = (f32[474]{0:T(512)S(1)}, f32[474]{0:T(512)}, u32[]{:S(2)}) copy-start(f32[474]{0:T(512)} %copy-done.46) | copy-start | bytes 5692
  1666.4 189.9 %all-gather.18.cloned.1.call-start = ((), (), s32[]{:S(2)}) async-start(), calls=%async_computation.19 | async-start | bytes 2949120 | tf_op jit(solution)/shard_map/all_gather | solution.py:227
  1698.7 161.0 %all-gather.16.cloned.1.call-start = ((), (), s32[]{:S(2)}) async-start(), calls=%async_computation.16 | async-start | bytes 2949120 | tf_op jit(solution)/shard_map/all_gather | solution.py:226
  1776.6 43.5 %copy-start.40 = (f32[474]{0:T(512)S(1)}, f32[474]{0:T(512)}, u32[]{:S(2)}) copy-start(f32[474]{0:T(512)} %copy-done.39) | copy-start | bytes 5692
  (57 other events, 399.0 us)
Sparse Core Ops, SparseCore 0:
  10.2 68.4 all-gather.7
  80.9 39.5 all-gather.9
  123.2 136.8 all-gather.13
  262.2 136.2 all-gather.11
  832.7 311.3 reduce-scatter.20
  1147.8 312.4 reduce-scatter.16
  1463.8 68.1 reduce-scatter.14
  1535.7 128.0 reduce-scatter.12
  1666.5 32.1 reduce-scatter.22
  1701.0 33.0 reduce-scatter.18
  1737.3 20.8 reduce-scatter.26
  1760.8 25.7 reduce-scatter.24
  1788.1 24.0 all-gather.17
  1813.6 24.1 all-gather.15
where the time goes:
time: 1880 us; the launch traced here: 1870 us
  waiting for transfers between devices  1130 us (60%)
  local copies, waits for them, and re-layouts  302 us (16%)
  matrix products  230 us (12%)
  blocking collectives  123 us (7%)
  other arithmetic  33.6 us (2%)
  loops' own time  30.4 us (2%)
    reduce_scatter x1, waiting for transfers between devices, per_device(): lax.psum_scatter(up_raw, 'fsdp', scatter_dimension=1, tiled=True)  316 us
    reduce_scatter x1, waiting for transfers between devices, per_device(): lax.psum_scatter(down_raw, 'fsdp', scatter_dimension=2, tiled=True)  256 us
    all_gather x1, waiting for transfers between devices, per_device(): lax.all_gather(w_down, 'fsdp', axis=2, tiled=True)  134 us
    reduce_scatter x1, waiting for transfers between devices, per_device(): lax.psum_scatter(qkv_weight_grad, 'fsdp', scatter_dimension=0, tiled=True)  130 us
    all_gather x1, waiting for transfers between devices, per_device(): lax.all_gather(w_up, 'fsdp', axis=1, tiled=True)  115 us
    dot_general x12, matrix products, contract_first(): lax.dot_general(left, right, (((0,), (0,)), ((), ())), preferred_element_...  107 us
    scatter-add x10, local copies, waits for them, and re-layouts, expert_backward(): down_total = down_total.at[expert].add(contract_first(act_low, block_grad))  91 us
    another operation x18, local copies, waits for them, and re-layouts  90.8 us
  transfers between devices with their start and end apart: 14, of which 10 were waited for; matrix products, arithmetic and copies ran while one was open for 8% of the time, Pallas kernels for 0%

commit v1 on v0

v1 whole, which is shorter than its diff:
```python
import functools

import jax
import jax.numpy as jnp
from jax import lax
from jax.experimental import pallas as pl
from jax.experimental.pallas import tpu as pltpu
from jax.sharding import PartitionSpec as P

HEADS = 12
HEAD = 64
TILE = 256
PATCHES = 197
MIB = 1024 * 1024
BF = jnp.bfloat16
F32 = jnp.float32


def dot(left, right, left_dim=1, right_dim=0):
    return lax.dot_general(
        left, right, (((left_dim,), (right_dim,)), ((), ())), preferred_element_type=F32
    )


def moments(values):
    center = values - jnp.mean(values, -1, keepdims=True)
    inverse = lax.rsqrt(jnp.mean(center * center, -1, keepdims=True) + 1e-06)
    return center * inverse, inverse


def norm_backward(grad, unit, inverse, gain):
    scaled = grad * gain
    slope = jnp.mean(scaled * unit, -1, keepdims=True)
    result = inverse * (scaled - jnp.mean(scaled, -1, keepdims=True) - unit * slope)
    return result, jnp.sum(grad * unit, 0, keepdims=True), jnp.sum(grad, 0, keepdims=True)


def gelu_parts(pre):
    share = 0.5 + 0.5 * lax.erf(pre * 0.7071067811865476)
    density = jnp.exp(-0.5 * pre * pre) * 0.3989422804014327
    return pre * share, share + pre * density


def run_copies(copies):
    for copy in copies:
        copy.start()
    for copy in copies:
        copy.wait()


def attention_copies(place, pieces, weights, sems, rows):
    copies = []
    for piece in pieces:
        for part in range(piece.shape[0]):
            at = len(copies)
            first = pl.multiple_of(place[2 * at + 1], 32)
            copies.append(
                pltpu.make_async_copy(
                    piece.at[part, pl.ds(0, rows)],
                    weights.at[place[2 * at], pl.ds(first, rows)],
                    sems.at[at],
                )
            )
    return copies


def tile(at):
    return pl.ds(pl.multiple_of(at * TILE, TILE), TILE)


def every(count, body):
    lax.fori_loop(0, count, lambda at, carry: (body(at), carry)[1], 0)


def attention_forward(rows, length, place, tok, gains, *refs):
    pieces, rest = refs[:-8], refs[-8:]
    first_in, qkv, probs, context, hidden, second_in, weights, sems = rest
    copies = attention_copies(place, pieces, weights, sems, rows)
    for copy in copies:
        copy.start()
    inputs = tok[...].astype(F32)
    padded, width = inputs.shape
    tiles = width // TILE
    unit, _ = moments(inputs)
    first_in[...] = (unit * gains[0:1] + gains[1:2]).astype(BF)
    for copy in copies:
        copy.wait()

    def project(at):
        block = weights[at // tiles, :, tile(at % tiles)]
        qkv[:, tile(at)] = dot(first_in[...], block).astype(BF)

    every(3 * tiles, project)
    pair = 2 * HEAD
    low_half = lax.broadcasted_iota(jnp.int32, (padded, pair), 1) < HEAD
    real = lax.broadcasted_iota(jnp.int32, (padded, padded), 1) < length

    def heads(at):
        lanes = pl.multiple_of(at * pair, pair)
        query = qkv[:, pl.ds(lanes, pair)]
        key = qkv[:, pl.ds(width + lanes, pair)]
        value = qkv[:, pl.ds(2 * width + lanes, pair)]
        total = jnp.zeros((padded, pair), F32)
        for half in range(2):
            keep = low_half if half == 0 else jnp.logical_not(low_half)
            scores = dot(jnp.where(keep, query, 0), key, 1, 1) * HEAD ** (-0.5)
            scores = jnp.where(real, scores, -1e30)
            grown = jnp.exp(scores - jnp.max(scores, -1, keepdims=True))
            prob = (grown / jnp.sum(grown, -1, keepdims=True)).astype(BF)
            probs[2 * at + half] = prob
            total += dot(prob, jnp.where(keep, value, 0))
        context[:, pl.ds(lanes, pair)] = total.astype(BF)

    every(HEADS // 2, heads)

    def project_out(at):
        added = dot(context[...], weights[3, :, tile(at)])
        hidden[:, tile(at)] = tok[:, tile(at)].astype(F32) + added

    every(tiles, project_out)
    unit, _ = moments(hidden[...])
    second_in[...] = (unit * gains[2:3] + gains[3:4]).astype(BF)


def block_copies(sources, target, sems, main, tail, first=0):
    copies = []
    for at, source in enumerate(sources):
        left = source.shape[0] - tail
        copies.append(
            pltpu.make_async_copy(
                source.at[pl.ds(0, main)], target.at[at], sems.at[first + 2 * at]
            )
        )
        copies.append(
            pltpu.make_async_copy(
                source.at[pl.ds(tail, left)],
                target.at[len(sources), pl.ds(at * left, left)],
                sems.at[first + 2 * at + 1],
            )
        )
    return copies


def expert_copies(place, pieces, weights, sems):
    copies = []
    for at, piece in enumerate(pieces):
        first = pl.multiple_of(place[at], 32)
        copies.append(
            pltpu.make_async_copy(
                piece, weights.at[:, pl.ds(first, piece.shape[1])], sems.at[at]
            )
        )
    return copies


def expert_layer(half, main, tail, place, kinds, *refs):
    states, grads = refs[:4], refs[4:8]
    pieces, rest = refs[8:-14], refs[-14:]
    act, dpre, keep_grad, send_grad, keep_out, send_out = rest[:6]
    weights, state, grad, state_out, grad_out, sems, state_sems, grad_sems = rest[6:]
    width, hidden = weights.shape[1:]
    left = keep_grad.shape[1] - tail
    copies = expert_copies(place, pieces, weights, sems)
    copies += block_copies(states, state, state_sems, main, tail)
    copies += block_copies([ref.at[half] for ref in grads], grad, grad_sems, main, tail)
    for copy in copies:
        copy.start()
    spare = main - 4 * left
    state[4, 4 * left :] = jnp.zeros((spare, width), BF)
    grad[4, 4 * left :] = jnp.zeros((spare, width), BF)
    for copy in copies:
        copy.wait()
    spot = lax.broadcasted_iota(jnp.int32, (main, 1), 0)
    image = spot < PATCHES
    text = (spot % left + tail >= PATCHES) & (spot < 4 * left)
    tiles = hidden // TILE

    def forward(step):
        at, columns = step // tiles, tile(step % tiles)
        expert = kinds[at]
        pre = dot(state[at], weights[expert, :, columns])
        dact = dot(grad[at], weights[2 + expert, :, columns])
        value, slope = gelu_parts(pre)
        mine = (image & (at < 4)) | (text & (at == 4))
        act[at, :, columns] = jnp.where(mine, value, 0).astype(BF)
        dpre[at, :, columns] = jnp.where(mine, dact * slope, 0).astype(BF)

    every(5 * tiles, forward)
    wide = width // TILE

    def outputs(step):
        at, columns = step // wide, tile(step % wide)
        expert = kinds[at]
        grad_out[at, :, columns] = dot(dpre[at], weights[expert, columns], 1, 1).astype(BF)
        state_out[at, :, columns] = dot(act[at], weights[2 + expert, columns], 1, 1).astype(BF)

    every(5 * wide, outputs)
    for rel in range(4):
        for source, target in (
            (grad_out, send_grad if rel % 2 else keep_grad),
            (state_out, send_out if rel % 2 else keep_out),
        ):
            target[rel // 2, :tail] = source[rel, :tail]
            both = source[4, rel * left : rel * left + main - tail]
            target[rel // 2, tail:main] = source[rel, tail:main] + both
            rest_rows = source[4, rel * left + main - tail : (rel + 1) * left]
            target[rel // 2, main:] = rest_rows


def expert_weight_grads(main, tail, halves, pieces, place, kinds, *refs):
    states, refs = refs[: 4 * halves], refs[4 * halves :]
    grads, refs = refs[:4], refs[4:]
    acts, refs = refs[:halves], refs[halves:]
    dpres, refs = refs[:halves], refs[halves:]
    outs, rest = refs[:pieces], refs[pieces:]
    total, rounded, state, grad, act, dpre, sems, state_sems, grad_sems, rest_sems = rest
    width, hidden = total.shape[1:]
    blocks = 5 * halves
    left = states[0].shape[0] - tail
    copies = []
    for half in range(halves):
        there = pl.ds(5 * half, 5)
        copies += block_copies(
            states[4 * half : 4 * half + 4], state.at[there], state_sems, main, tail, 8 * half
        )
        copies += block_copies(
            [ref.at[half] for ref in grads], grad.at[there], grad_sems, main, tail, 8 * half
        )
        copies.append(pltpu.make_async_copy(acts[half], act.at[there], rest_sems.at[2 * half]))
        copies.append(
            pltpu.make_async_copy(dpres[half], dpre.at[there], rest_sems.at[2 * half + 1])
        )
    for copy in copies:
        copy.start()
    for half in range(halves):
        spare = main - 4 * left
        state[5 * half + 4, 4 * left :] = jnp.zeros((spare, width), BF)
        grad[5 * half + 4, 4 * left :] = jnp.zeros((spare, width), BF)
    total[...] = jnp.zeros(total.shape, F32)
    for copy in copies:
        copy.wait()
    tiles = width // TILE

    def accumulate(step):
        at, columns = step // tiles, tile(step % tiles)
        expert = kinds[at]
        total[expert, columns] += dot(state[at, :, columns], dpre[at], 0, 0)
        total[2 + expert, columns] += dot(grad[at, :, columns], act[at], 0, 0)

    every(blocks * tiles, accumulate)
    rounded[...] = total[...].astype(BF)
    copies = []
    for at, out in enumerate(outs):
        first = pl.multiple_of(place[at], 32)
        copies.append(
            pltpu.make_async_copy(rounded.at[:, pl.ds(first, out.shape[1])], out, sems.at[at])
        )
    run_copies(copies)


def attention_backward(rows, length, place, tok, gains, near, far, dmixed, qkv, probs, hidden, *refs):
    pieces, rest = refs[:-7], refs[-7:]
    low, dqkv, input_grad, norm_grads, weights, total, sems = rest
    copies = attention_copies(place, pieces, weights, sems, rows)
    for copy in copies:
        copy.start()
    padded, width = tok.shape
    tiles = width // TILE
    unit, inverse = moments(hidden[...])
    second = near[...].astype(F32) + far[...].astype(F32)
    part, gain_two, bias_two = norm_backward(second, unit, inverse, gains[2:3])
    low[...] = (dmixed[...].astype(F32) + part).astype(BF)
    norm_grads[2:3] = gain_two
    norm_grads[3:4] = bias_two
    for copy in copies:
        copy.wait()

    def project_out(at):
        dqkv[:, tile(at)] = dot(low[...], weights[3, tile(at)], 1, 1).astype(BF)

    every(tiles, project_out)
    pair = 2 * HEAD
    low_half = lax.broadcasted_iota(jnp.int32, (padded, pair), 1) < HEAD

    def heads(at):
        lanes = pl.multiple_of(at * pair, pair)
        query = qkv[:, pl.ds(lanes, pair)]
        key = qkv[:, pl.ds(width + lanes, pair)]
        value = qkv[:, pl.ds(2 * width + lanes, pair)]
        upper = dqkv[:, pl.ds(lanes, pair)]
        dquery = jnp.zeros((padded, pair), F32)
        dkey = jnp.zeros((padded, pair), F32)
        dvalue = jnp.zeros((padded, pair), F32)
        for half in range(2):
            keep = low_half if half == 0 else jnp.logical_not(low_half)
            prob = probs[2 * at + half]
            wide = prob.astype(F32)
            upper_half = jnp.where(keep, upper, 0)
            dprob = dot(upper_half, value, 1, 1)
            dscore = (wide * (dprob - jnp.sum(dprob * wide, -1, keepdims=True))).astype(BF)
            dquery += dot(dscore, jnp.where(keep, key, 0))
            dkey += dot(dscore, jnp.where(keep, query, 0), 0, 0)
            dvalue += dot(prob, upper_half, 0, 0)
        dqkv[:, pl.ds(lanes, pair)] = (dquery * HEAD ** (-0.5)).astype(BF)
        dqkv[:, pl.ds(width + lanes, pair)] = (dkey * HEAD ** (-0.5)).astype(BF)
        dqkv[:, pl.ds(2 * width + lanes, pair)] = dvalue.astype(BF)

    every(HEADS // 2, heads)

    def project(at):
        part = dot(dqkv[:, 0:width], weights[0, tile(at)], 1, 1)
        part += dot(dqkv[:, width : 2 * width], weights[1, tile(at)], 1, 1)
        part += dot(dqkv[:, 2 * width : 3 * width], weights[2, tile(at)], 1, 1)
        total[:, tile(at)] = part

    every(tiles, project)
    unit, inverse = moments(tok[...].astype(F32))
    part, gain_one, bias_one = norm_backward(total[...], unit, inverse, gains[0:1])
    norm_grads[0:1] = gain_one
    norm_grads[1:2] = bias_one
    unit, inverse = moments(hidden[...])
    second = near[...].astype(F32) + far[...].astype(F32)
    upper, _, _ = norm_backward(second, unit, inverse, gains[2:3])
    input_grad[...] = (part + (dmixed[...].astype(F32) + upper))[:length]


def attention_weight_grads(halves, rows, extra, parts, place, *refs):
    firsts, refs = refs[:halves], refs[halves:]
    contexts, refs = refs[:halves], refs[halves:]
    lows, refs = refs[:halves], refs[halves:]
    dqkvs, refs = refs[:halves], refs[halves:]
    norms, refs = refs[:halves], refs[halves:]
    keep, send, rounded, vectors, sems = refs
    width = firsts[0].shape[1]
    tiles = width // TILE

    def project(step):
        part, columns = step // tiles, tile(step % tiles)
        there = pl.ds(pl.multiple_of(part * width, width), width)
        total = dot(firsts[0][:, columns], dqkvs[0][:, there], 0, 0)
        for first, dqkv in zip(firsts[1:], dqkvs[1:]):
            total += dot(first[:, columns], dqkv[:, there], 0, 0)
        rounded[part, columns] = total.astype(BF)

    every(3 * tiles, project)

    def project_out(step):
        columns = tile(step)
        total = dot(contexts[0][:, columns], lows[0][...], 0, 0)
        for context, low in zip(contexts[1:], lows[1:]):
            total += dot(context[:, columns], low[...], 0, 0)
        rounded[3, columns] = total.astype(BF)

    every(tiles, project_out)
    if extra:
        norm = norms[0][...]
        for ref in norms[1:]:
            norm += ref[...]
        spot = lax.broadcasted_iota(jnp.int32, (extra, width), 0)
        lane = lax.broadcasted_iota(jnp.int32, (extra, width), 1)
        inside = (spot == 0) & (lane < rows)
        for part in range(4):
            for shard in range(width // rows):
                row = jnp.broadcast_to(norm[part : part + 1], (extra, width))
                if shard:
                    row = pltpu.roll(row, width - shard * rows, 1)
                vectors[part, shard] = jnp.where(inside, row, 0.0).astype(BF)
    copies = []
    for at in range(4 * parts):
        side, index = divmod(at, 2 * parts)
        ref = keep if side == 0 else send
        outer, inner = divmod(index, parts)
        quarter, shard = place[2 * at], place[2 * at + 1]
        first_row = pl.multiple_of(shard * rows, 32)
        copies.append(
            pltpu.make_async_copy(
                rounded.at[quarter, pl.ds(first_row, rows)],
                ref.at[outer, inner, pl.ds(0, rows)],
                sems.at[len(copies)],
            )
        )
        if extra:
            copies.append(
                pltpu.make_async_copy(
                    vectors.at[quarter, shard],
                    ref.at[outer, inner, pl.ds(rows, extra)],
                    sems.at[len(copies)],
                )
            )
    run_copies(copies)


ANYWHERE = pl.BlockSpec(memory_space=pl.ANY)
SCALARS = pl.BlockSpec(memory_space=pltpu.SMEM)
WHOLE = pl.BlockSpec(memory_space=pltpu.VMEM)


def one_of(array, index):
    tail = (0,) * (array.ndim - 1)
    return pl.BlockSpec((None,) + array.shape[1:], lambda step: (index,) + tail)


def shaped(shape, dtype=BF):
    return jax.ShapeDtypeStruct(shape, dtype)


def call(kernel, out_shape, in_specs, out_specs, scratch, args, flops, moved):
    return pl.pallas_call(
        kernel,
        grid=(1,),
        out_shape=out_shape,
        in_specs=in_specs,
        out_specs=out_specs,
        scratch_shapes=scratch,
        compiler_params=pltpu.CompilerParams(vmem_limit_bytes=50 * MIB),
        cost_estimate=pl.CostEstimate(flops=flops, bytes_accessed=moved, transcendentals=0),
    )(*args)


def add(left, right):
    return (left.astype(F32) + right.astype(F32)).astype(BF)


def per_device(
    tokens,
    token_type,
    mlm_mask,
    cotangent,
    ln1_gain,
    ln1_bias,
    w_qkv,
    w_out,
    ln2_gain,
    ln2_bias,
    w_up,
    w_down,
):
    halves, length, width = tokens.shape
    shards, replicas = lax.axis_size("fsdp"), lax.axis_size("dp")
    shard, replica = lax.axis_index("fsdp"), lax.axis_index("dp")
    rows = width // shards
    lines = shards // 2
    line, side = shard // 2, shard % 2
    columns = w_up.shape[2] // replicas
    padded = -(-length // 16) * 16
    main = -(-PATCHES // 16) * 16
    tail = PATCHES // 16 * 16
    ringed = rows % 32 == 0
    extra = 16 if ringed else 0
    spans = rows if ringed else width

    def swap(axis, size, bit):
        return lambda value: lax.ppermute(value, axis, [(i, i ^ bit) for i in range(size)])

    swap_core = swap("dp", replicas, 1)
    swap_row = swap("dp", replicas, 2)
    swap_side = swap("fsdp", shards, 1)

    def step_line(value):
        return lax.ppermute(value, "fsdp", [(i, (i + 2) % shards) for i in range(shards)])

    def owner(steps, other):
        return 2 * jnp.mod(line - steps, lines) + jnp.bitwise_xor(side, other)

    order = [(steps, other) for steps in range(lines) for other in range(2)]

    block = jnp.where(
        replica < 3,
        lax.dynamic_slice(w_qkv, (0, jnp.minimum(replica, 2) * width), (rows, width)),
        w_out,
    )
    vectors = jnp.stack([ln1_gain, ln1_bias, ln2_gain, ln2_bias])
    if ringed:
        line_block = jnp.zeros((extra, width), BF).at[0, : 4 * rows].set(vectors.reshape(-1))
        block = jnp.concatenate([block, line_block], 0)
        held = jnp.stack([block, swap_side(block)])
        ring = [held]
        for _ in range(lines - 1):
            ring.append(step_line(ring[-1]))
        found = jnp.concatenate([part[:, rows, : 4 * rows] for part in ring], 0)
        wanted = jnp.arange(shards)
        found = found[
            2 * jnp.mod(line - wanted // 2, lines) + jnp.bitwise_xor(wanted % 2, side)
        ]
        gains = found.reshape(shards, 4, rows).transpose(1, 0, 2).reshape(4, width)
    else:
        ring = [lax.all_gather(block, "fsdp", axis=0, tiled=True)[None]]
        gains = lax.all_gather(vectors, "fsdp", axis=1, tiled=True)
    gains = gains.astype(F32)
    attn_pieces, attn_place = [], []
    for steps, part in enumerate(ring):
        across = swap_row(part)
        for rel, copy in enumerate((part, swap_core(part), across, swap_core(across))):
            attn_pieces.append(copy)
            for other in range(part.shape[0]):
                attn_place.append(jnp.bitwise_xor(replica, rel))
                attn_place.append(owner(steps, other) * rows if ringed else jnp.int32(0))
    attn_place = jnp.stack(attn_place).astype(jnp.int32)

    expert_block = jnp.concatenate(
        [
            lax.dynamic_slice(w_up, (0, 0, replica * columns), (2, rows, columns)),
            lax.dynamic_slice(w_down, (0, replica * columns, 0), (2, columns, rows)).transpose(
                0, 2, 1
            ),
        ],
        0,
    )
    if ringed:
        expert_pieces, current = [], expert_block
        for steps in range(lines):
            expert_pieces += [current, swap_side(current)]
            if steps < lines - 1:
                current = step_line(current)
        expert_place = jnp.stack([owner(*at) * rows for at in order]).astype(jnp.int32)
    else:
        expert_pieces = [lax.all_gather(expert_block, "fsdp", axis=1, tiled=True)]
        expert_place = jnp.zeros((1,), jnp.int32)

    kinds_here = token_type[:, 0]
    image_count = jnp.sum(mlm_mask * token_type)
    counts = jnp.stack([jnp.sum(mlm_mask) - image_count, image_count])
    bits = jnp.sum(kinds_here << jnp.arange(halves))

    def note(bits_now, counts_now):
        return jnp.zeros((8, 128), jnp.int32).at[0, :3].set(
            jnp.concatenate([bits_now[None], counts_now])
        )

    heard = swap_core(note(bits, counts))[0]
    bits, counts = bits | (heard[0] << halves), counts + heard[1:3]
    heard = swap_row(note(bits, counts))[0]
    bits, counts = bits | (heard[0] << (2 * halves)), counts + heard[1:3]
    stride = 1
    while stride < shards:
        heard = swap("fsdp", shards, stride)(note(bits, counts))[0]
        counts = counts + heard[1:3]
        stride *= 2
    kinds = (bits >> jnp.arange(4 * halves)) & 1
    kinds = kinds.reshape(4, halves).T
    kinds = jnp.concatenate([kinds, jnp.zeros((halves, 1), jnp.int32)], 1)

    gap = ((0, 0), (0, padded - length), (0, 0))
    tok = jnp.pad(tokens, gap)
    dmixed = jnp.pad(cotangent * mlm_mask[..., None].astype(BF), gap)
    dmixed_row = swap_row(dmixed)
    grads = [dmixed, swap_core(dmixed), dmixed_row, swap_core(dmixed_row)]

    attn_sems = pltpu.SemaphoreType.DMA((attn_place.shape[0] // 2,))
    attn_weights = pltpu.VMEM((4, width, width), BF)
    states_of, kept = [], []
    for half in range(halves):
        first_in, qkv, probs, context, hidden, second_in = call(
            functools.partial(attention_forward, spans, length),
            [
                shaped((padded, width)),
                shaped((padded, 3 * width)),
                shaped((HEADS, padded, padded)),
                shaped((padded, width)),
                shaped((padded, width), F32),
                shaped((padded, width)),
            ],
            [SCALARS, one_of(tok, half), WHOLE] + [ANYWHERE] * len(attn_pieces),
            [WHOLE] * 6,
            [attn_weights, attn_sems],
            (attn_place, tok, gains, *attn_pieces),
            flops=10 * padded * width * width,
            moved=16 * MIB,
        )
        kept.append((first_in, qkv, probs, context, hidden))
        across = swap_row(second_in)
        states_of.append([second_in, swap_core(second_in), across, swap_core(across)])

    expert_scratch = [
        pltpu.VMEM((4, width, columns), BF),
        *[pltpu.VMEM((5, main, width), BF)] * 4,
        pltpu.SemaphoreType.DMA((len(expert_pieces),)),
        pltpu.SemaphoreType.DMA((8,)),
        pltpu.SemaphoreType.DMA((8,)),
    ]
    acts, dpres, outs, arriving = [], [], [], []
    for half in range(halves):
        act, dpre, keep_grad, send_grad, keep_out, send_out = call(
            functools.partial(expert_layer, half, main, tail),
            [shaped((5, main, columns))] * 2 + [shaped((2, padded, width))] * 4,
            [SCALARS] * 2 + [ANYWHERE] * (8 + len(expert_pieces)),
            [WHOLE] * 6,
            expert_scratch,
            (expert_place, kinds[half], *states_of[half], *grads, *expert_pieces),
            flops=32 * padded * width * columns,
            moved=16 * MIB,
        )
        acts.append(act)
        dpres.append(dpre)
        summed = add(keep_grad, swap_core(send_grad))
        arriving.append((summed, swap_row(summed[1])))
        outs.append(add(keep_out, swap_core(send_out)))

    piece_count = len(expert_pieces)
    expert_parts = call(
        functools.partial(expert_weight_grads, main, tail, halves, piece_count),
        [shaped((4, spans, columns))] * piece_count,
        [SCALARS] * 2 + [ANYWHERE] * (4 * halves + 4 + 2 * halves),
        [ANYWHERE] * piece_count,
        [
            pltpu.VMEM((4, width, columns), F32),
            pltpu.VMEM((4, width, columns), BF),
            *[pltpu.VMEM((5 * halves, main, width), BF)] * 2,
            *[pltpu.VMEM((5 * halves, main, columns), BF)] * 2,
            pltpu.SemaphoreType.DMA((piece_count,)),
            pltpu.SemaphoreType.DMA((8 * halves,)),
            pltpu.SemaphoreType.DMA((8 * halves,)),
            pltpu.SemaphoreType.DMA((2 * halves,)),
        ],
        (
            expert_place,
            kinds.reshape(-1),
            *[state for states in states_of for state in states],
            *grads,
            *acts,
            *dpres,
        ),
        flops=32 * padded * width * columns,
        moved=16 * MIB,
    )

    if ringed:
        near = {}
        for steps in [*range(1, lines), 0]:
            near[steps] = add(expert_parts[2 * steps], swap_side(expert_parts[2 * steps + 1]))
        current = near[1]
        for steps in range(1, lines):
            current = add(step_line(current), near[(steps + 1) % lines])
    else:
        current = lax.psum_scatter(expert_parts[0], "fsdp", scatter_dimension=1, tiled=True)

    def all_replicas(value):
        across = swap_row(value)
        return jnp.stack([value, swap_core(value), across, swap_core(across)])

    def in_order(found):
        return [
            lax.dynamic_index_in_dim(found, jnp.bitwise_xor(replica, at), 0, keepdims=False)
            for at in range(4)
        ]

    expert_all = in_order(all_replicas(current))
    divisor = counts.astype(F32)[:, None, None]
    up_grad = jnp.concatenate([part[:2] for part in expert_all], 2).astype(F32) / divisor
    down_grad = (
        jnp.concatenate([part[2:] for part in expert_all], 2).astype(F32).transpose(0, 2, 1)
        / divisor
    )

    out_sum = jnp.stack(outs)
    out_rest = swap_row(out_sum[:, 1])
    mixed = jnp.stack(
        [
            (kept[h][4] + out_sum[h, 0].astype(F32) + out_rest[h].astype(F32))[:length]
            for h in range(halves)
        ]
    ).astype(BF)

    lows, dqkvs, norm_parts, input_grads = [], [], [], []
    for half in range(halves):
        first_in, qkv, probs, context, hidden = kept[half]
        summed, far = arriving[half]
        low, dqkv, input_grad, norm_grads = call(
            functools.partial(attention_backward, spans, length),
            [
                shaped((padded, width)),
                shaped((padded, 3 * width)),
                shaped((length, width), F32),
                shaped((4, width), F32),
            ],
            [SCALARS, one_of(tok, half), WHOLE, one_of(summed, 0), WHOLE, one_of(dmixed, half)]
            + [WHOLE] * 3
            + [ANYWHERE] * len(attn_pieces),
            [WHOLE] * 4,
            [attn_weights, pltpu.VMEM((padded, width), F32), attn_sems],
            (attn_place, tok, gains, summed, far, dmixed, qkv, probs, hidden, *attn_pieces),
            flops=20 * padded * width * width,
            moved=16 * MIB,
        )
        lows.append(low)
        dqkvs.append(dqkv)
        norm_parts.append(norm_grads)
        input_grads.append(input_grad)
    input_grad = jnp.stack(input_grads)

    parts = shards if ringed else 1
    grad_place = []
    for core in range(2):
        for row in range(2):
            if ringed:
                spots = [owner(steps, other) for other in range(2) for steps in range(lines)]
            else:
                spots = [jnp.int32(0)]
            for spot in spots:
                grad_place += [jnp.bitwise_xor(replica, 2 * row + core), spot]
    grad_place = jnp.stack(grad_place).astype(jnp.int32)
    keep, send = call(
        functools.partial(attention_weight_grads, halves, spans, extra, parts),
        [shaped((2, parts, spans + extra, width))] * 2,
        [SCALARS] + [WHOLE] * (5 * halves),
        [ANYWHERE] * 2,
        [
            pltpu.VMEM((4, width, width), BF),
            pltpu.VMEM((4, parts, max(extra, 16), width), BF),
            pltpu.SemaphoreType.DMA((8 * parts,)),
        ],
        (
            grad_place,
            *[kept[h][0] for h in range(halves)],
            *[kept[h][3] for h in range(halves)],
            *lows,
            *dqkvs,
            *norm_parts,
        ),
        flops=8 * halves * padded * width * width,
        moved=16 * MIB,
    )
    summed = add(keep, swap_core(send))
    summed = add(summed[0], swap_row(summed[1]))
    if ringed:
        summed = summed.reshape(2, lines, spans + extra, width)
        summed = add(summed[0], swap_side(summed[1]))
        current = summed[1 % lines]
        for steps in range(1, lines):
            current = add(step_line(current), summed[(steps + 1) % lines])
        attn_all = in_order(all_replicas(current))
        vector_grads = [part[rows, :rows].astype(F32) for part in attn_all]
    else:
        current = lax.psum_scatter(summed[0], "fsdp", scatter_dimension=0, tiled=True)
        attn_all = in_order(all_replicas(current))
        norm_sum = functools.reduce(jnp.add, norm_parts)
        norm_sum = lax.psum_scatter(norm_sum, "fsdp", scatter_dimension=1, tiled=True)
        vector_grads = list(lax.psum(norm_sum, "dp"))
    attn_all = [part[:rows].astype(F32) for part in attn_all]
    return (
        mixed,
        input_grad,
        vector_grads[0],
        vector_grads[1],
        jnp.concatenate(attn_all[:3], 1),
        attn_all[3],
        vector_grads[2],
        vector_grads[3],
        up_grad,
        down_grad,
        counts,
    )


def solution(mesh):
    return jax.shard_map(
        per_device,
        mesh=mesh,
        in_specs=(
            P(("fsdp", "dp"), None, None),
            P(("fsdp", "dp"), None),
            P(("fsdp", "dp"), None),
            P(("fsdp", "dp"), None, None),
            P("fsdp"),
            P("fsdp"),
            P("fsdp", None),
            P("fsdp", None),
            P("fsdp"),
            P("fsdp"),
            P(None, "fsdp", None),
            P(None, None, "fsdp"),
        ),
        out_specs=(
            P(("fsdp", "dp"), None, None),
            P(("fsdp", "dp"), None, None),
            P("fsdp"),
            P("fsdp"),
            P("fsdp", None),
            P("fsdp", None),
            P("fsdp"),
            P("fsdp"),
            P(None, "fsdp", None),
            P(None, None, "fsdp"),
            P(),
        ),
        check_vma=False,
    )
```

time: 1880 us -> 380 us (0.20)
  waiting for transfers between devices: 1130 us -> 143 us
  local copies, waits for them, and re-layouts: 302 us -> 21 us
  matrix products: 230 us -> 0 us
  Pallas kernels: 0 us -> 139 us
  blocking collectives: 123 us -> 0 us
  starting transfers between devices: 0.56 us -> 48.7 us
  loops' own time: 30.4 us -> 0 us
    reduce_scatter x6 -> x0, waiting for transfers between devices: 841 us -> none  [the longest x1 316 us: per_device(): lax.psum_scatter(up_raw, 'fsdp', scatter_dimension=1, tiled=True)]
    all_gather x6 -> x0, waiting for transfers between devices: 289 us -> none  [the longest x1 134 us: per_device(): lax.all_gather(w_down, 'fsdp', axis=2, tiled=True)]
    dot_general x42 -> x0, matrix products: 230 us -> none  [the longest x12 107 us: contract_first(): lax.dot_general(left, right, (((0,), (0,)), ((), ())), preferred_element_...]
    ppermute x0 -> x63, waiting for transfers between devices: none -> 143 us  [the longest x51 99.2 us: swap(): lax.ppermute(value, axis, [(i, i ^ bit) for i in range(size)])]
    pallas_call x0 -> x8, Pallas kernels: none -> 139 us  [call(): pl.pallas_call(kernel, grid=(1,), out_shape=out_shape, in_specs=in_specs,...]
    scatter-add x10 -> x0, local copies, waits for them, and re-layouts: 91 us -> none  [expert_backward(): down_total = down_total.at[expert].add(contract_first(act_low, block_grad))]
    another operation x18 -> x4, local copies, waits for them, and re-layouts: 90.8 us -> 0.47 us  [the longest x1 0.15 us: per_device(): grad_place = jnp.stack(grad_place).astype(jnp.int32)]
    unnamed x2 -> x0, blocking collectives: 60.8 us -> none
  transfers between devices with their start and end apart: 14 -> 63, of which waited for: 10 -> 23; matrix products, arithmetic and copies ran while one was open for 8% -> 8% of each run, Pallas kernels for 0% -> 29%
where the time goes in v1:
time: 380 us; the launch traced here: 379 us
  waiting for transfers between devices  143 us (38%)
  Pallas kernels  139 us (37%)
  starting transfers between devices  48.7 us (13%)
  other arithmetic  22.6 us (6%)
  local copies, waits for them, and re-layouts  21 us (6%)
  between operations  4.78 us (1%)
    pallas_call x8, Pallas kernels, call(): pl.pallas_call(kernel, grid=(1,), out_shape=out_shape, in_specs=in_specs,...  139 us
    ppermute x51, waiting for transfers between devices, swap(): lax.ppermute(value, axis, [(i, i ^ bit) for i in range(size)])  99.2 us
    ppermute x12, waiting for transfers between devices, step_line(): lax.ppermute(value, 'fsdp', [(i, (i + 2) % shards) for i in range(shards)])  43.8 us
    ppermute x51, starting transfers between devices, swap(): lax.ppermute(value, axis, [(i, i ^ bit) for i in range(size)])  36.1 us
    ppermute x12, starting transfers between devices, step_line(): lax.ppermute(value, 'fsdp', [(i, (i + 2) % shards) for i in range(shards)])  12.6 us
    unnamed x90, local copies, waits for them, and re-layouts  11.4 us
  transfers between devices with their start and end apart: 63, of which 23 were waited for; matrix products, arithmetic and copies ran while one was open for 8% of the time, Pallas kernels for 29%

profile of v1, /device:TPU:0, one launch (start us, length us, event | category | flops | bytes accessed | tf_op | source)
XLA Modules:
  0.0 378.9 jit_solution(17606537992522173090)
XLA Ops:
  9.2 2.5 collective-permute-start
  23.6 17.9 %collective-permute-done.17 = s32[8,128]{1,0:T(8,128)S(1)} collective-permute-done((s32[8,128]{1,0:T(8,128)S(1)}, s32[8,128]{1,0:T(8,128)S(1)}, u32[]{:S(2)}, u32[]{:S(2)}) %collective-permute-start.17) | collective-permute-done | bytes 4128 | tf_op jit(solution)/shard_map/ppermute | solution.py:453
  46.6 7.7 %collective-permute-done.2.refs_8_ = bf16[2,112,768]{2,1,0:T(8,128)(2,1)S(1)} collective-permute-done((bf16[2,112,768]{2,1,0:T(8,128)(2,1)S(1)}, bf16[2,112,768]{2,1,0:T(8,128)(2,1)S(1)}, u32[]{:S(2)}, u32[]{:S(2)}) %collective-permute-start.2) | collective-permute-done | bytes 344096 | tf_op jit(solution)/shard_map/ppermute | solution.py:460
  56.3 17.6 %collective-permute-done.3.refs_12_ = bf16[2,112,768]{2,1,0:T(8,128)(2,1)} collective-permute-done((bf16[2,112,768]{2,1,0:T(8,128)(2,1)S(1)}, bf16[2,112,768]{2,1,0:T(8,128)(2,1)}, u32[]{:S(2)}, u32[]{:S(2)}) %collective-permute-start.3) | collective-permute-done | bytes 344096 | tf_op jit(solution)/shard_map/ppermute | solution.py:460
  77.4 6.5 %collective-permute-done.14.refs_14_ = bf16[2,112,768]{2,1,0:T(8,128)(2,1)} collective-permute-done((bf16[2,112,768]{2,1,0:T(8,128)(2,1)}, bf16[2,112,768]{2,1,0:T(8,128)(2,1)}, u32[]{:S(2)}, u32[]{:S(2)}) %collective-permute-start.14) | collective-permute-done | bytes 344096 | tf_op jit(solution)/shard_map/ppermute | solution.py:453
  90.7 17.7 %shard_map.203 = (bf16[240,768]{1,0:T(8,128)(2,1)}, bf16[240,2304]{1,0:T(8,128)(2,1)}, bf16[12,240,240]{2,1,0:T(8,128)(2,1)}, bf16[240,768]{1,0:T(8,128)(2,1)}, ...) custom-call(s32[64]{0:T(128)S(1)} %stack.121.place, bf16[2,240,768]{2,1,0:T(8,128)(2,1)} %pad.33.tok, ...), custom_call_target="tpu_custom_call" | custom-call | flops 1415577600 | bytes 16777216 | tf_op jit(solution)/shard_map/pallas_call | solution.py:408
  112.0 17.5 %shard_map.205 = (bf16[240,768]{1,0:T(8,128)(2,1)}, bf16[240,2304]{1,0:T(8,128)(2,1)}, bf16[12,240,240]{2,1,0:T(8,128)(2,1)}, bf16[240,768]{1,0:T(8,128)(2,1)}, ...) custom-call(s32[64]{0:T(128)S(1)} %stack.121.place, bf16[2,240,768]{2,1,0:T(8,128)(2,1)} %pad.33.tok, ...), custom_call_target="tpu_custom_call" | custom-call | flops 1415577600 | bytes 16777216 | tf_op jit(solution)/shard_map/pallas_call | solution.py:408
  132.7 6.7 %collective-permute-done.33.refs_2_.refs_6_ = bf16[240,768]{1,0:T(8,128)(2,1)} collective-permute-done((bf16[240,768]{1,0:T(8,128)(2,1)}, bf16[240,768]{1,0:T(8,128)(2,1)}, u32[]{:S(2)}, u32[]{:S(2)}) %collective-permute-start.33) | collective-permute-done | bytes 368672 | tf_op jit(solution)/shard_map/ppermute | solution.py:453
  140.5 18.7 %shard_map.204 = (bf16[5,208,768]{2,1,0:T(8,128)(2,1)}, bf16[5,208,768]{2,1,0:T(8,128)(2,1)}, bf16[2,240,768]{2,1,0:T(8,128)(2,1)}, bf16[2,240,768]{2,1,0:T(8,12...) custom-call(s32[8]{0:T(128)S(1)} %stack.130.place, s32[5]{0:T(128)S(1)} %get-tuple-element.249.kinds, ...), custom_call_target="tpu_custom_call" | custom-call | flops 4529848320 | bytes 16777216 | tf_op jit(solution)/shard_map/pallas_call | solution.py:408
  159.8 18.6 %shard_map.206 = (bf16[5,208,768]{2,1,0:T(8,128)(2,1)}, bf16[5,208,768]{2,1,0:T(8,128)(2,1)}, bf16[2,240,768]{2,1,0:T(8,128)(2,1)}, bf16[2,240,768]{2,1,0:T(8,12...) custom-call(s32[8]{0:T(128)S(1)} %stack.130.place, s32[5]{0:T(128)S(1)} %get-tuple-element.250.kinds, ...), custom_call_target="tpu_custom_call" | custom-call | flops 4529848320 | bytes 16777216 | tf_op jit(solution)/shard_map/pallas_call | solution.py:408
  182.7 8.5 %collective-permute-done.38.far = bf16[240,768]{1,0:T(8,128)(2,1)} collective-permute-done((bf16[240,768]{1,0:T(8,128)(2,1)}, bf16[240,768]{1,0:T(8,128)(2,1)}, u32[]{:S(2)}, u32[]{:S(2)}) %collective-permute-start.38) | collective-permute-done | bytes 368672 | tf_op jit(solution)/shard_map/ppermute | solution.py:453
  192.2 18.3 %shard_map.207 = (bf16[240,768]{1,0:T(8,128)(2,1)}, bf16[240,2304]{1,0:T(8,128)(2,1)}, f32[237,768]{1,0:T(8,128)}, f32[4,768]{1,0:T(4,128)S(1)}) custom-call(s32[64]{0:T(128)S(1)} %stack.121.place, bf16[2,240,768]{2,1,0:T(8,128)(2,1)} %pad.33.tok, f32[4,768]{1,0:T(4,128)S(1)} %reshape.412.gains, bf16[2,240,768]{2,1,0:T(8,128)(2,1)} %copy-done.22, ...), custom_call_target="tpu_custom_call" | custom-call | flops 2831155200 | bytes 16777216 | tf_op jit(solution)/shard_map/pallas_call | solution.py:408
  210.6 18.7 %shard_map.208 = (bf16[240,768]{1,0:T(8,128)(2,1)}, bf16[240,2304]{1,0:T(8,128)(2,1)}, f32[237,768]{1,0:T(8,128)}, f32[4,768]{1,0:T(4,128)S(1)}) custom-call(s32[64]{0:T(128)S(1)} %stack.121.place, bf16[2,240,768]{2,1,0:T(8,128)(2,1)} %pad.33.tok, f32[4,768]{1,0:T(4,128)S(1)} %reshape.412.gains, bf16[2,240,768]{2,1,0:T(8,128)(2,1)} %copy-done.21, ...), custom_call_target="tpu_custom_call" | custom-call | flops 2831155200 | bytes 16777216 | tf_op jit(solution)/shard_map/pallas_call | solution.py:408
  230.4 9.2 %shard_map.209 = (bf16[2,8,112,768]{3,2,1,0:T(8,128)(2,1)}, bf16[2,8,112,768]{3,2,1,0:T(8,128)(2,1)}) custom-call(s32[64]{0:T(128)S(1)} %stack.151.place, bf16[240,768]{1,0:T(8,128)(2,1)S(1)} %copy-done.11, bf16[240,768]{1,0:T(8,128)(2,1)S(1)} %copy-done.15, bf16[240,768]{1,0:T(8,128)(2,1)S(1)} %copy-done.12, bf16[240,768]{1,0:T(8,128)(2,1)S(1)} %copy-done.16, ...), custom_call_target="tpu_custom_call" | custom-call | flops 2264924160 | bytes 16777216 | tf_op jit(solution)/shard_map/pallas_call | solution.py:408
  244.8 20.2 %shard_map.210 = (bf16[4,96,768]{2,1,0:T(8,128)(2,1)S(1)}, bf16[4,96,768]{2,1,0:T(8,128)(2,1)}, bf16[4,96,768]{2,1,0:T(8,128)(2,1)}, bf16[4,96,768]{2,1,0:T(8,12...) custom-call(s32[8]{0:T(128)S(1)} %stack.130.place, ...), custom_call_target="tpu_custom_call" | custom-call | flops 4529848320 | bytes 16777216 | tf_op jit(solution)/shard_map/pallas_call | solution.py:408
  267.6 2.6 collective-permute-done.61
  272.4 2.5 collective-permute-done.62
  277.6 3.3 collective-permute-done.50
  285.3 3.3 add_convert_fusion
  288.7 4.8 %collective-permute-done.52 = bf16[4,96,768]{2,1,0:T(8,128)(2,1)S(1)} collective-permute-done((bf16[4,96,768]{2,1,0:T(8,128)(2,1)}, bf16[4,96,768]{2,1,0:T(8,128)(2,1)S(1)}, u32[]{:S(2)}, u32[]{:S(2)}) %collective-permute-start.52) | collective-permute-done | bytes 589856 | tf_op jit(solution)/shard_map/ppermute | solution.py:453
  293.5 4.3 %collective-permute-done.51 = bf16[4,96,768]{2,1,0:T(8,128)(2,1)S(1)} collective-permute-done((bf16[4,96,768]{2,1,0:T(8,128)(2,1)S(1)}, bf16[4,96,768]{2,1,0:T(8,128)(2,1)S(1)}, u32[]{:S(2)}, u32[]{:S(2)}) %collective-permute-start.51) | collective-permute-done | bytes 589856 | tf_op jit(solution)/shard_map/ppermute | solution.py:460
  299.9 6.3 %collective-permute-done.54 = bf16[4,96,768]{2,1,0:T(8,128)(2,1)S(1)} collective-permute-done((bf16[4,96,768]{2,1,0:T(8,128)(2,1)}, bf16[4,96,768]{2,1,0:T(8,128)(2,1)S(1)}, u32[]{:S(2)}, u32[]{:S(2)}) %collective-permute-start.54) | collective-permute-done | bytes 589856 | tf_op jit(solution)/shard_map/ppermute | solution.py:453
  306.1 5.6 %collective-permute-done.53 = bf16[4,96,768]{2,1,0:T(8,128)(2,1)S(1)} collective-permute-done((bf16[4,96,768]{2,1,0:T(8,128)(2,1)S(1)}, bf16[4,96,768]{2,1,0:T(8,128)(2,1)S(1)}, u32[]{:S(2)}, u32[]{:S(2)}) %collective-permute-start.53) | collective-permute-done | bytes 589856 | tf_op jit(solution)/shard_map/ppermute | solution.py:460
  312.0 14.1 %collective-permute-done.42 = bf16[8,112,768]{2,1,0:T(8,128)(2,1)S(1)} collective-permute-done((bf16[8,112,768]{2,1,0:T(8,128)(2,1)S(1)}, bf16[8,112,768]{2,1,0:T(8,128)(2,1)S(1)}, u32[]{:S(2)}, u32[]{:S(2)}) %collective-permute-start.42) | collective-permute-done | bytes 1376288 | tf_op jit(solution)/shard_map/ppermute | solution.py:453
  326.5 2.3 collective-permute-start.43
  333.7 7.7 %collective-permute-done.43 = bf16[4,112,768]{2,1,0:T(8,128)(2,1)S(1)} collective-permute-done((bf16[4,112,768]{2,1,0:T(8,128)(2,1)S(1)}, bf16[4,112,768]{2,1,0:T(8,128)(2,1)S(1)}, u32[]{:S(2)}, u32[]{:S(2)}) %collective-permute-start.43) | collective-permute-done | bytes 688160 | tf_op jit(solution)/shard_map/ppermute | solution.py:453
  341.6 2.8 collective-permute-start.44
  344.4 4.0 %collective-permute-done.36 = bf16[2,240,768]{2,1,0:T(8,128)(2,1)S(1)} collective-permute-done((bf16[2,240,768]{2,1,0:T(8,128)(2,1)S(1)}, bf16[2,240,768]{2,1,0:T(8,128)(2,1)S(1)}, u32[]{:S(2)}, u32[]{:S(2)}) %collective-permute-start.36) | collective-permute-done | bytes 737312 | tf_op jit(solution)/shard_map/ppermute | solution.py:453
  350.6 6.1 %collective-permute-done.58 = bf16[4,96,768]{2,1,0:T(8,128)(2,1)S(1)} collective-permute-done((bf16[4,96,768]{2,1,0:T(8,128)(2,1)S(1)}, bf16[4,96,768]{2,1,0:T(8,128)(2,1)S(1)}, u32[]{:S(2)}, u32[]{:S(2)}) %collective-permute-start.58) | collective-permute-done | bytes 589856 | tf_op jit(solution)/shard_map/ppermute | solution.py:453
  361.2 5.9 %collective-permute-done.46 = bf16[112,768]{1,0:T(8,128)(2,1)S(1)} collective-permute-done((bf16[112,768]{1,0:T(8,128)(2,1)S(1)}, bf16[112,768]{1,0:T(8,128)(2,1)S(1)}, u32[]{:S(2)}, u32[]{:S(2)}) %collective-permute-start.46) | collective-permute-done | bytes 172064 | tf_op jit(solution)/shard_map/ppermute | solution.py:460
  368.2 5.2 %collective-permute-done.48 = bf16[112,768]{1,0:T(8,128)(2,1)S(1)} collective-permute-done((bf16[112,768]{1,0:T(8,128)(2,1)S(1)}, bf16[112,768]{1,0:T(8,128)(2,1)S(1)}, u32[]{:S(2)}, u32[]{:S(2)}) %collective-permute-start.48) | collective-permute-done | bytes 172064 | tf_op jit(solution)/shard_map/ppermute | solution.py:453
  373.4 2.5 divide_bitcast_fusion
  (274 shorter events, 84.7 us)
Async XLA Ops:
  12.8 30.6 %collective-permute-start.25 = (bf16[4,96,768]{2,1,0:T(8,128)(2,1)S(1)}, bf16[4,96,768]{2,1,0:T(8,128)(2,1)}, u32[]{:S(2)}, u32[]{:S(2)}) collective-permute-start(bf16[4,96,768]{2,1,0:T(8,128)(2,1)S(1)} %pad_maximum_fusion.5.refs_8_), channel_id=1, source_target_pairs={{0,8},{4,12},{8,16},{12,20},{16,24},{20,28},{24,0},{28,4},{1,9},{5... | collective-permute-start | bytes 1769480 | tf_op jit(solution)/shard_map/ppermute | solution.py:460
  15.5 31.1 %collective-permute-start.22 = (bf16[2,240,768]{2,1,0:T(8,128)(2,1)}, bf16[2,240,768]{2,1,0:T(8,128)(2,1)}, u32[]{:S(2)}, u32[]{:S(2)}) collective-permute-start(bf16[2,240,768]{2,1,0:T(8,128)(2,1)} %pad.34.refs_4_.dmixed.refs_8_), channel_id=1, source_target_pairs={{0,2},{1,3},{2,0},{3,1},{4,6},{5,7},{6,4},{7,5},{8,10},{9,11},{10,... | collective-permute-start | bytes 2211848 | tf_op jit(solution)/shard_map/ppermute | solution.py:453
  17.1 24.4 %collective-permute-start.1 = (bf16[2,112,768]{2,1,0:T(8,128)(2,1)S(1)}, bf16[2,112,768]{2,1,0:T(8,128)(2,1)S(1)}, u32[]{:S(2)}, u32[]{:S(2)}) collective-permute-start(bf16[2,112,768]{2,1,0:T(8,128)(2,1)S(1)} %pad_maximum_fusion.6.refs_0_), channel_id=1, source_target_pairs={{0,8},{4,12},{8,16},{12,20},{16,24},{20,28},{24,0},{28,4},{1,9},{5... | collective-permute-start | bytes 1032200 | tf_op jit(solution)/shard_map/ppermute | solution.py:460
  20.7 22.5 %collective-permute-start.5 = (bf16[2,112,768]{2,1,0:T(8,128)(2,1)S(1)}, bf16[2,112,768]{2,1,0:T(8,128)(2,1)S(1)}, u32[]{:S(2)}, u32[]{:S(2)}) collective-permute-start(bf16[2,112,768]{2,1,0:T(8,128)(2,1)S(1)} %pad_maximum_fusion.6.refs_0_), channel_id=1, source_target_pairs={{0,2},{1,3},{2,0},{3,1},{4,6},{5,7},{6,4},{7,5},{8,10},{9,11},{10,... | collective-permute-start | bytes 1032200 | tf_op jit(solution)/shard_map/ppermute | solution.py:453
  23.1 18.4 %collective-permute-start.17 = (s32[8,128]{1,0:T(8,128)S(1)}, s32[8,128]{1,0:T(8,128)S(1)}, u32[]{:S(2)}, u32[]{:S(2)}) collective-permute-start(s32[8,128]{1,0:T(8,128)S(1)} %scatter.24), channel_id=1, source_target_pairs={{0,2},{1,3},{2,0},{3,1},{4,6},{5,7},{6,4},{7,5},{8,10},{9,11},{10,... | collective-permute-start | bytes 12296 | tf_op jit(solution)/shard_map/ppermute | solution.py:453
  43.4 32.1 %collective-permute-start.27 = (bf16[4,96,768]{2,1,0:T(8,128)(2,1)}, bf16[4,96,768]{2,1,0:T(8,128)(2,1)}, u32[]{:S(2)}, u32[]{:S(2)}) collective-permute-start(bf16[4,96,768]{2,1,0:T(8,128)(2,1)} %collective-permute-done.25.refs_10_), channel_id=1, source_target_pairs={{0,8},{4,12},{8,16},{12,20},{16,24},{20,28},{24,0},{28,4},{1,9},{5... | collective-permute-start | bytes 1769480 | tf_op jit(solution)/shard_map/ppermute | solution.py:460
  54.2 19.7 %collective-permute-start.3 = (bf16[2,112,768]{2,1,0:T(8,128)(2,1)S(1)}, bf16[2,112,768]{2,1,0:T(8,128)(2,1)}, u32[]{:S(2)}, u32[]{:S(2)}) collective-permute-start(bf16[2,112,768]{2,1,0:T(8,128)(2,1)S(1)} %collective-permute-done.2.refs_8_), channel_id=1, source_target_pairs={{0,8},{4,12},{8,16},{12,20},{16,24},{20,28},{24,0},{28,4},{1,9},{5... | collective-permute-start | bytes 1032200 | tf_op jit(solution)/shard_map/ppermute | solution.py:460
  54.2 21.3 %collective-permute-start.11 = (bf16[2,112,768]{2,1,0:T(8,128)(2,1)S(1)}, bf16[2,112,768]{2,1,0:T(8,128)(2,1)S(1)}, u32[]{:S(2)}, u32[]{:S(2)}) collective-permute-start(bf16[2,112,768]{2,1,0:T(8,128)(2,1)S(1)} %collective-permute-done.2.refs_8_), channel_id=1, source_target_pairs={{0,2},{1,3},{2,0},{3,1},{4,6},{5,7},{6,4},{7,5},{8,10},{9,11},{10,... | collective-permute-start | bytes 1032200 | tf_op jit(solution)/shard_map/ppermute | solution.py:453
  55.8 20.2 %collective-permute-start.9 = (bf16[2,112,768]{2,1,0:T(8,128)(2,1)S(1)}, bf16[2,112,768]{2,1,0:T(8,128)(2,1)S(1)}, u32[]{:S(2)}, u32[]{:S(2)}) collective-permute-start(bf16[2,112,768]{2,1,0:T(8,128)(2,1)S(1)} %collective-permute-done.8.refs_6_), channel_id=1, source_target_pairs={{0,1},{1,0},{2,3},{3,2},{4,5},{5,4},{6,7},{7,6},{8,9},{9,8},{10,11... | collective-permute-start | bytes 1032200 | tf_op jit(solution)/shard_map/ppermute | solution.py:453
  55.8 20.2 %collective-permute-start.10 = (bf16[2,112,768]{2,1,0:T(8,128)(2,1)S(1)}, bf16[2,112,768]{2,1,0:T(8,128)(2,1)S(1)}, u32[]{:S(2)}, u32[]{:S(2)}) collective-permute-start(bf16[2,112,768]{2,1,0:T(8,128)(2,1)S(1)} %collective-permute-done.2.refs_8_), channel_id=1, source_target_pairs={{0,1},{1,0},{2,3},{3,2},{4,5},{5,4},{6,7},{7,6},{8,9},{9,8},{10,11... | collective-permute-start | bytes 1032200 | tf_op jit(solution)/shard_map/ppermute | solution.py:453
  76.0 34.0 %collective-permute-start.21 = (bf16[2,240,768]{2,1,0:T(8,128)(2,1)}, bf16[2,240,768]{2,1,0:T(8,128)(2,1)}, u32[]{:S(2)}, u32[]{:S(2)}) collective-permute-start(bf16[2,240,768]{2,1,0:T(8,128)(2,1)} %pad.34.refs_4_.dmixed.refs_8_), channel_id=1, source_target_pairs={{0,1},{1,0},{2,3},{3,2},{4,5},{5,4},{6,7},{7,6},{8,9},{9,8},{10,11... | collective-permute-start | bytes 2211848 | tf_op jit(solution)/shard_map/ppermute | solution.py:453
  76.8 31.5 %collective-permute-start.24 = (bf16[4,96,768]{2,1,0:T(8,128)(2,1)}, bf16[4,96,768]{2,1,0:T(8,128)(2,1)}, u32[]{:S(2)}, u32[]{:S(2)}) collective-permute-start(bf16[4,96,768]{2,1,0:T(8,128)(2,1)} %copy-done.5), channel_id=1, source_target_pairs={{0,4},{4,0},{8,12},{12,8},{16,20},{20,16},{24,28},{28,24},{1,5},{5... | collective-permute-start | bytes 1769480 | tf_op jit(solution)/shard_map/ppermute | solution.py:453
  83.9 46.2 %collective-permute-start.23 = (bf16[2,240,768]{2,1,0:T(8,128)(2,1)}, bf16[2,240,768]{2,1,0:T(8,128)(2,1)}, u32[]{:S(2)}, u32[]{:S(2)}) collective-permute-start(bf16[2,240,768]{2,1,0:T(8,128)(2,1)} %collective-permute-done.22.refs_6_.refs_10_), channel_id=1, source_target_pairs={{0,1},{1,0},{2,3},{3,2},{4,5},{5,4},{6,7},{7,6},{8,9},{9,8},{10,11... | collective-permute-start | bytes 2211848 | tf_op jit(solution)/shard_map/ppermute | solution.py:453
  84.5 27.1 %collective-permute-start.29 = (bf16[4,96,768]{2,1,0:T(8,128)(2,1)}, bf16[4,96,768]{2,1,0:T(8,128)(2,1)}, u32[]{:S(2)}, u32[]{:S(2)}) collective-permute-start(bf16[4,96,768]{2,1,0:T(8,128)(2,1)} %collective-permute-done.27.refs_12_), channel_id=1, source_target_pairs={{0,8},{4,12},{8,16},{12,20},{16,24},{20,28},{24,0},{28,4},{1,9},{5... | collective-permute-start | bytes 1769480 | tf_op jit(solution)/shard_map/ppermute | solution.py:460
  88.3 41.3 %collective-permute-start.26 = (bf16[4,96,768]{2,1,0:T(8,128)(2,1)}, bf16[4,96,768]{2,1,0:T(8,128)(2,1)}, u32[]{:S(2)}, u32[]{:S(2)}) collective-permute-start(bf16[4,96,768]{2,1,0:T(8,128)(2,1)} %collective-permute-done.25.refs_10_), channel_id=1, source_target_pairs={{0,4},{4,0},{8,12},{12,8},{16,20},{20,16},{24,28},{28,24},{1,5},{5... | collective-permute-start | bytes 1769480 | tf_op jit(solution)/shard_map/ppermute | solution.py:453
  108.4 21.7 %collective-permute-start.19 = (bf16[240,768]{1,0:T(8,128)(2,1)}, bf16[240,768]{1,0:T(8,128)(2,1)}, u32[]{:S(2)}, u32[]{:S(2)}) collective-permute-start(bf16[240,768]{1,0:T(8,128)(2,1)} %get-tuple-element.126.refs_0_), channel_id=1, source_target_pairs={{0,2},{1,3},{2,0},{3,1},{4,6},{5,7},{6,4},{7,5},{8,10},{9,11},{10,... | collective-permute-start | bytes 1105928 | tf_op jit(solution)/shard_map/ppermute | solution.py:453
  110.0 22.5 %collective-permute-start.28 = (bf16[4,96,768]{2,1,0:T(8,128)(2,1)}, bf16[4,96,768]{2,1,0:T(8,128)(2,1)}, u32[]{:S(2)}, u32[]{:S(2)}) collective-permute-start(bf16[4,96,768]{2,1,0:T(8,128)(2,1)} %collective-permute-done.27.refs_12_), channel_id=1, source_target_pairs={{0,4},{4,0},{8,12},{12,8},{16,20},{20,16},{24,28},{28,24},{1,5},{5... | collective-permute-start | bytes 1769480 | tf_op jit(solution)/shard_map/ppermute | solution.py:453
  111.5 27.9 %collective-permute-start.30 = (bf16[4,96,768]{2,1,0:T(8,128)(2,1)}, bf16[4,96,768]{2,1,0:T(8,128)(2,1)}, u32[]{:S(2)}, u32[]{:S(2)}) collective-permute-start(bf16[4,96,768]{2,1,0:T(8,128)(2,1)} %collective-permute-done.29.refs_14_), channel_id=1, source_target_pairs={{0,4},{4,0},{8,12},{12,8},{16,20},{20,16},{24,28},{28,24},{1,5},{5... | collective-permute-start | bytes 1769480 | tf_op jit(solution)/shard_map/ppermute | solution.py:453
  132.6 27.2 %collective-permute-start.32 = (bf16[240,768]{1,0:T(8,128)(2,1)}, bf16[240,768]{1,0:T(8,128)(2,1)S(1)}, u32[]{:S(2)}, u32[]{:S(2)}) collective-permute-start(bf16[240,768]{1,0:T(8,128)(2,1)} %get-tuple-element.129.refs_0_.refs_4_), channel_id=1, source_target_pairs={{0,1},{1,0},{2,3},{3,2},{4,5},{5,4},{6,7},{7,6},{8,9},{9,8},{10,11... | collective-permute-start | bytes 1105928 | tf_op jit(solution)/shard_map/ppermute | solution.py:453
  139.4 20.4 %collective-permute-start.34 = (bf16[240,768]{1,0:T(8,128)(2,1)}, bf16[240,768]{1,0:T(8,128)(2,1)S(1)}, u32[]{:S(2)}, u32[]{:S(2)}) collective-permute-start(bf16[240,768]{1,0:T(8,128)(2,1)} %collective-permute-done.33.refs_2_.refs_6_), channel_id=1, source_target_pairs={{0,1},{1,0},{2,3},{3,2},{4,5},{5,4},{6,7},{7,6},{8,9},{9,8},{10,11... | collective-permute-start | bytes 1105928 | tf_op jit(solution)/shard_map/ppermute | solution.py:453
  159.2 19.3 %collective-permute-start.37 = (bf16[2,240,768]{2,1,0:T(8,128)(2,1)}, bf16[2,240,768]{2,1,0:T(8,128)(2,1)S(1)}, u32[]{:S(2)}, u32[]{:S(2)}) collective-permute-start(bf16[2,240,768]{2,1,0:T(8,128)(2,1)} %get-tuple-element.134), channel_id=1, source_target_pairs={{0,1},{1,0},{2,3},{3,2},{4,5},{5,4},{6,7},{7,6},{8,9},{9,8},{10,11... | collective-permute-start | bytes 2211848 | tf_op jit(solution)/shard_map/ppermute | solution.py:453
  181.9 28.6 %collective-permute-start.40 = (bf16[240,768]{1,0:T(8,128)(2,1)}, bf16[240,768]{1,0:T(8,128)(2,1)}, u32[]{:S(2)}, u32[]{:S(2)}) collective-permute-start(bf16[240,768]{1,0:T(8,128)(2,1)} %slice_bitcast_fusion.2), channel_id=1, source_target_pairs={{0,2},{1,3},{2,0},{3,1},{4,6},{5,7},{6,4},{7,5},{8,10},{9,11},{10,... | collective-permute-start | bytes 1105928 | tf_op jit(solution)/shard_map/ppermute | solution.py:453
  239.6 44.7 %collective-permute-start.41 = (bf16[2,8,112,768]{3,2,1,0:T(8,128)(2,1)}, bf16[2,8,112,768]{3,2,1,0:T(8,128)(2,1)}, u32[]{:S(2)}, u32[]{:S(2)}) collective-permute-start(bf16[2,8,112,768]{3,2,1,0:T(8,128)(2,1)} %get-tuple-element.154), channel_id=1, source_target_pairs={{0,1},{1,0},{2,3},{3,2},{4,5},{5,4},{6,7},{7,6},{8,9},{9,8},{10,11... | collective-permute-start | bytes 8257544 | tf_op jit(solution)/shard_map/ppermute | solution.py:453
  275.5 23.0 %collective-permute-start.31 = (bf16[2,240,768]{2,1,0:T(8,128)(2,1)S(1)}, bf16[2,240,768]{2,1,0:T(8,128)(2,1)S(1)}, u32[]{:S(2)}, u32[]{:S(2)}) collective-permute-start(bf16[2,240,768]{2,1,0:T(8,128)(2,1)S(1)} %copy-done.38), channel_id=1, source_target_pairs={{0,1},{1,0},{2,3},{3,2},{4,5},{5,4},{6,7},{7,6},{8,9},{9,8},{10,11... | collective-permute-start | bytes 2211848 | tf_op jit(solution)/shard_map/ppermute | solution.py:453
  275.5 18.0 %collective-permute-start.52 = (bf16[4,96,768]{2,1,0:T(8,128)(2,1)}, bf16[4,96,768]{2,1,0:T(8,128)(2,1)S(1)}, u32[]{:S(2)}, u32[]{:S(2)}) collective-permute-start(bf16[4,96,768]{2,1,0:T(8,128)(2,1)} %get-tuple-element.162), channel_id=1, source_target_pairs={{0,4},{4,0},{8,12},{12,8},{16,20},{20,16},{24,28},{28,24},{1,5},{5... | collective-permute-start | bytes 1769480 | tf_op jit(solution)/shard_map/ppermute | solution.py:453
  276.1 30.1 %collective-permute-start.54 = (bf16[4,96,768]{2,1,0:T(8,128)(2,1)}, bf16[4,96,768]{2,1,0:T(8,128)(2,1)S(1)}, u32[]{:S(2)}, u32[]{:S(2)}) collective-permute-start(bf16[4,96,768]{2,1,0:T(8,128)(2,1)} %get-tuple-element.164), channel_id=1, source_target_pairs={{0,4},{4,0},{8,12},{12,8},{16,20},{20,16},{24,28},{28,24},{1,5},{5... | collective-permute-start | bytes 1769480 | tf_op jit(solution)/shard_map/ppermute | solution.py:453
  280.8 51.6 %collective-permute-start.56 = (bf16[4,96,768]{2,1,0:T(8,128)(2,1)}, bf16[4,96,768]{2,1,0:T(8,128)(2,1)S(1)}, u32[]{:S(2)}, u32[]{:S(2)}) collective-permute-start(bf16[4,96,768]{2,1,0:T(8,128)(2,1)} %get-tuple-element.166), channel_id=1, source_target_pairs={{0,4},{4,0},{8,12},{12,8},{16,20},{20,16},{24,28},{28,24},{1,5},{5... | collective-permute-start | bytes 1769480 | tf_op jit(solution)/shard_map/ppermute | solution.py:453
  297.8 28.3 %collective-permute-start.42 = (bf16[8,112,768]{2,1,0:T(8,128)(2,1)S(1)}, bf16[8,112,768]{2,1,0:T(8,128)(2,1)S(1)}, u32[]{:S(2)}, u32[]{:S(2)}) collective-permute-start(bf16[8,112,768]{2,1,0:T(8,128)(2,1)S(1)} %slice_bitcast_fusion), channel_id=1, source_target_pairs={{0,2},{1,3},{2,0},{3,1},{4,6},{5,7},{6,4},{7,5},{8,10},{9,11},{10,... | collective-permute-start | bytes 4128776 | tf_op jit(solution)/shard_map/ppermute | solution.py:453
  312.0 20.5 %collective-permute-start.55 = (bf16[4,96,768]{2,1,0:T(8,128)(2,1)S(1)}, bf16[4,96,768]{2,1,0:T(8,128)(2,1)S(1)}, u32[]{:S(2)}, u32[]{:S(2)}) collective-permute-start(bf16[4,96,768]{2,1,0:T(8,128)(2,1)S(1)} %add_convert_fusion.8), channel_id=1, source_target_pairs={{0,8},{4,12},{8,16},{12,20},{16,24},{20,28},{24,0},{28,4},{1,9},{5... | collective-permute-start | bytes 1769480 | tf_op jit(solution)/shard_map/ppermute | solution.py:460
  328.9 19.5 %collective-permute-start.36 = (bf16[2,240,768]{2,1,0:T(8,128)(2,1)S(1)}, bf16[2,240,768]{2,1,0:T(8,128)(2,1)S(1)}, u32[]{:S(2)}, u32[]{:S(2)}) collective-permute-start(bf16[2,240,768]{2,1,0:T(8,128)(2,1)S(1)} %fusion.6), channel_id=1, source_target_pairs={{0,2},{1,3},{2,0},{3,1},{4,6},{5,7},{6,4},{7,5},{8,10},{9,11},{10,... | collective-permute-start | bytes 2211848 | tf_op jit(solution)/shard_map/ppermute | solution.py:453
  332.7 23.9 %collective-permute-start.58 = (bf16[4,96,768]{2,1,0:T(8,128)(2,1)S(1)}, bf16[4,96,768]{2,1,0:T(8,128)(2,1)S(1)}, u32[]{:S(2)}, u32[]{:S(2)}) collective-permute-start(bf16[4,96,768]{2,1,0:T(8,128)(2,1)S(1)} %add_convert_fusion.6), channel_id=1, source_target_pairs={{0,2},{1,3},{2,0},{3,1},{4,6},{5,7},{6,4},{7,5},{8,10},{9,11},{10,... | collective-permute-start | bytes 1769480 | tf_op jit(solution)/shard_map/ppermute | solution.py:453
  350.5 17.1 %collective-permute-start.57 = (bf16[4,96,768]{2,1,0:T(8,128)(2,1)S(1)}, bf16[4,96,768]{2,1,0:T(8,128)(2,1)S(1)}, u32[]{:S(2)}, u32[]{:S(2)}) collective-permute-start(bf16[4,96,768]{2,1,0:T(8,128)(2,1)S(1)} %add_convert_fusion.6), channel_id=1, source_target_pairs={{0,1},{1,0},{2,3},{3,2},{4,5},{5,4},{6,7},{7,6},{8,9},{9,8},{10,11... | collective-permute-start | bytes 1769480 | tf_op jit(solution)/shard_map/ppermute | solution.py:453
  (71 other events, 746.4 us)
